TPU v7x, 128 devices: a whole 4x4x4 slice. The times are simulated.
128 devices in a mesh: rows: 32 (over y, x, core), cols: 4 (over z).
Axes of the slice: x: 4, y: 4, z: 4, core: 2. Of those that a mesh axis runs over, the one named last changes fastest.
Arguments:
- embeddings: bfloat16 [262144, 2048], P('rows', 'cols'), may hold values from -6 to 6
- pick_rows: int32 [2, 32], replicated, may hold values from 0 to 262143, as said below
Outputs:
- residual: float32 [262144, 2048], P('rows', 'cols')
Inputs may be any that keep to these rules, and one draw needn't show every extreme that they name: `pick_rows`: all 64 indices are distinct; the picks of one round fall on the row owners as evenly as their count allows.
All inputs are finite; a program needn't handle non-finite values.
Results may differ from a plain program's by a relative error of at most 0.0003.
Values sent between devices are 32-bit elements; how exact they have to be, the bound alone decides.
No kernel may reach another device: no remote copies, remote signals or barrier semaphores. Data moves between devices by JAX's collectives and lax.ppermute only.
A program may use at most 128 MiB of HBM per device.

v0:
```python
import jax
import jax.numpy as jnp
from jax import lax
from jax.sharding import PartitionSpec as P

HIGH = lax.Precision.HIGHEST


def orthonormal_panel(pick_panel):
    gram_matrix = jnp.dot(
        pick_panel, pick_panel.T, precision=HIGH, preferred_element_type=jnp.float32
    )
    factor = jnp.linalg.cholesky(gram_matrix)
    return jax.scipy.linalg.solve_triangular(factor, pick_panel, lower=True)


def gather_panel(residual, wanted):
    row_count, width_part = residual.shape
    first_row = lax.axis_index("rows") * row_count
    local_index = jnp.clip(wanted - first_row, 0, row_count - 1)
    owned = (wanted >= first_row) & (wanted < first_row + row_count)
    taken = jnp.take(residual, local_index, axis=0)
    partial_panel = jnp.where(owned[:, None], taken, jnp.zeros_like(taken))
    summed = lax.psum(partial_panel, "rows")
    return lax.all_gather(summed, "cols", axis=1, tiled=True)


def column_part(basis_rows, width_part):
    return lax.dynamic_slice_in_dim(basis_rows, lax.axis_index("cols") * width_part, width_part, 1)


def per_device(embeddings, pick_rows):
    residual = embeddings.astype(jnp.float32)
    width_part = residual.shape[1]
    rounds_total = pick_rows.shape[0]
    for round_index in range(rounds_total):
        pick_panel = gather_panel(residual, pick_rows[round_index])
        local_basis = column_part(orthonormal_panel(pick_panel), width_part)
        partial_weights = jnp.dot(
            residual, local_basis.T, precision=HIGH, preferred_element_type=jnp.float32
        )
        weights = lax.psum(partial_weights, "cols")
        residual = residual - jnp.dot(
            weights, local_basis, precision=HIGH, preferred_element_type=jnp.float32
        )
    return residual


def solution(mesh):
    in_specs = (P("rows", "cols"), P())
    out_specs = P("rows", "cols")
    return jax.shard_map(
        per_device, mesh=mesh, in_specs=in_specs, out_specs=out_specs, check_vma=False
    )
```

profile of v0, /device:TPU:0, one launch (start us, length us, event | category | flops | bytes accessed | tf_op | source)
XLA Modules:
  0.0 435.4 jit_solution(12734813438256048249)
XLA Ops:
  6.5 0.0 all-reduce.5.cloned.1.call-start
  6.5 0.8 compare_and_fusion
  7.3 0.8 and_bitcast_fusion
  8.1 12.0 %convert_element_type.3 = f32[8192,512]{1,0:T(8,128)} convert(bf16[8192,512]{1,0:T(8,128)(2,1)} %param.7) | non-fusion elementwise | flops 4194304 | bytes 25165824 | tf_op jit(solution)/shard_map/convert_element_type | solution.py:33
  20.0 6.4 %gather_fusion = f32[32,512]{1,0:T(8,128)S(1)} fusion(f32[8192,512]{1,0:T(8,128)} %convert_element_type.3, s32[1024]{0:T(1024)S(1)} %pad_clamp_fusion.1), kind=kCustom, calls=%fused_computation.clone | custom fusion | bytes 131200 | tf_op jit(solution)/shard_map/jit(_take)/gather | solution.py:22
  26.4 0.7 select_select_fusion.1
  27.1 0.0 all-reduce.5.cloned.1.call-update
  27.2 0.0 all-reduce.7.cloned.1.call-start
  27.2 97.9 %all-reduce.5.cloned.1.call-done = f32[32,512]{1,0:T(8,128)} async-done(((f32[32,512]{1,0:T(8,128)}), f32[32,512]{1,0:T(8,128)}) %all-reduce.5.cloned.1.call-update) | async-done | bytes 65552 | tf_op jit(solution)/shard_map/psum | solution.py:24
  125.2 13.1 %all_gather.6 = f32[32,2048]{1,0:T(8,128)S(1)} all-gather(f32[32,512]{1,0:T(8,128)} %all-reduce.5.cloned.1.call-done), channel_id=1, replica_groups=mesh['rows'=32,'cols'=4] {'cols'}, dimensions={1}, use_global_device_ids=true | all-gather | bytes 327680 | tf_op jit(solution)/shard_map/all_gather | solution.py:25
  138.2 0.3 fusion.17
  138.6 0.1 copy.5
  138.7 2.9 cholesky.44
  141.6 0.6 compare_reduce_fusion.1
  142.3 0.7 fusion.5
  142.9 2.4 custom-call.6
  145.3 0.4 fusion.10
  145.8 10.5 %convolution_bitcast_fusion = f32[8192,32]{0,1:T(8,128)} fusion(bf16[8192,512]{1,0:T(8,128)(2,1)} %param.7, f32[32,2048]{1,0:T(8,128)S(1)} %fusion.10, s32[]{:T(128)S(6)} %select_n.22), kind=kOutput, calls=%fused_computation.4 | convolution fusion | flops 1610612736 | bytes 9502724 | tf_op jit(solution)/shard_map/dot_general | solution.py:39
  156.3 0.0 all-reduce.7.cloned.1.call-update
  156.4 0.0 all-reduce.9.cloned.1.call-start
  156.4 44.4 %all-reduce.7.cloned.1.call-done = f32[8192,32]{0,1:T(8,128)} async-done(((f32[8192,32]{0,1:T(8,128)}), f32[8192,32]{0,1:T(8,128)}) %all-reduce.7.cloned.1.call-update) | async-done | bytes 1048592 | tf_op jit(solution)/shard_map/psum | solution.py:42
  200.8 18.6 %convolution_subtract_fusion.1 = f32[8192,512]{1,0:T(8,128)} fusion(f32[8192,32]{0,1:T(8,128)} %all-reduce.7.cloned.1.call-done, bf16[8192,512]{1,0:T(8,128)(2,1)} %param.7, f32[32,2048]{1,0:T(8,128)S(1)} %fusion.10, s32[]{:T(128)S(6)} %select_n.22), kind=kOutput, calls=%fused_computation.3 | convolution fusion | flops 1619001344 | bytes 26279940 | tf_op jit(solution)/shard_map/dot_general | solution.py:43
  219.4 6.4 %gather_fusion.1 = f32[32,512]{1,0:T(8,128)S(1)} fusion(f32[8192,512]{1,0:T(8,128)} %convolution_subtract_fusion.1, s32[1024]{0:T(1024)S(1)} %pad_clamp_fusion), kind=kCustom, calls=%fused_computation.1.clone | custom fusion | bytes 131200 | tf_op jit(solution)/shard_map/jit(_take)/gather | solution.py:22
  225.8 0.7 select_select_fusion
  226.5 0.0 all-reduce.9.cloned.1.call-update
  226.5 0.0 all-reduce.11.cloned.1.call-start
  226.6 96.2 %all-reduce.9.cloned.1.call-done = f32[32,512]{1,0:T(8,128)} async-done(((f32[32,512]{1,0:T(8,128)}), f32[32,512]{1,0:T(8,128)}) %all-reduce.9.cloned.1.call-update) | async-done | bytes 65552 | tf_op jit(solution)/shard_map/psum | solution.py:24
  322.8 13.2 %all_gather.7 = f32[32,2048]{1,0:T(8,128)S(1)} all-gather(f32[32,512]{1,0:T(8,128)} %all-reduce.9.cloned.1.call-done), channel_id=1, replica_groups=mesh['rows'=32,'cols'=4] {'cols'}, dimensions={1}, use_global_device_ids=true | all-gather | bytes 327680 | tf_op jit(solution)/shard_map/all_gather | solution.py:25
  336.1 0.3 fusion.18
  336.4 0.1 copy.6
  336.5 2.9 cholesky.55
  339.4 0.7 compare_reduce_fusion
  340.2 0.7 fusion.6
  340.9 2.4 custom-call.7
  343.3 0.4 fusion.7
  343.8 19.9 %fusion.1 = f32[8192,32]{0,1:T(8,128)} fusion(f32[8192,512]{1,0:T(8,128)} %convolution_subtract_fusion.1, f32[32,2048]{1,0:T(8,128)S(1)} %fusion.7, s32[]{:T(128)S(6)} %select_n.22), kind=kOutput, calls=%fused_computation.8 | convolution fusion | flops 1610612736 | bytes 17891332 | tf_op jit(solution)/shard_map/dot_general | solution.py:39
  363.7 0.0 all-reduce.11.cloned.1.call-update
  363.7 44.4 %all-reduce.11.cloned.1.call-done = f32[8192,32]{0,1:T(8,128)} async-done(((f32[8192,32]{0,1:T(8,128)}), f32[8192,32]{0,1:T(8,128)}) %all-reduce.11.cloned.1.call-update) | async-done | bytes 1048592 | tf_op jit(solution)/shard_map/psum | solution.py:42
  408.1 20.7 %convolution_subtract_fusion = f32[8192,512]{1,0:T(8,128)} fusion(f32[8192,512]{1,0:T(8,128)} %convolution_subtract_fusion.1, f32[8192,32]{0,1:T(8,128)} %all-reduce.11.cloned.1.call-done, f32[32,2048]{1,0:T(8,128)S(1)} %fusion.7, s32[]{:T(128)S(6)} %select_n.22), kind=kOutput, calls=%fused_computation.2 | convolution fusion | flops 1614807040 | bytes 34668548 | tf_op jit(solution)/shard_map/dot_general | solution.py:43
  (6 shorter events, 0.1 us)
Async XLA Ops:
  6.5 118.6 %all-reduce.5.cloned.1.call-start = ((), (), s32[]{:S(2)}) async-start(), calls=%async_computation | async-start | bytes 131072 | tf_op jit(solution)/shard_map/psum | solution.py:24
  27.2 173.6 %all-reduce.7.cloned.1.call-start = ((), (), s32[]{:S(2)}) async-start(), calls=%async_computation.1 | async-start | bytes 2097152 | tf_op jit(solution)/shard_map/psum | solution.py:42
  156.4 166.4 %all-reduce.9.cloned.1.call-start = ((), (), s32[]{:S(2)}) async-start(), calls=%async_computation.2 | async-start | bytes 131072 | tf_op jit(solution)/shard_map/psum | solution.py:24
  226.5 181.6 %all-reduce.11.cloned.1.call-start = ((), (), s32[]{:S(2)}) async-start(), calls=%async_computation.3 | async-start | bytes 2097152 | tf_op jit(solution)/shard_map/psum | solution.py:42
Sparse Core Ops, SparseCore 0:
  27.3 97.8 all-reduce.4
  156.5 44.2 all-reduce.6
  226.6 96.1 all-reduce.8
  363.8 44.2 all-reduce.10
where the time goes:
time: 436 us; the launch traced here: 435 us
  waiting for transfers between devices  283 us (65%)
  matrix products  71.4 us (16%)
  other arithmetic  28.4 us (7%)
  blocking collectives  26.3 us (6%)
  between operations  13.2 us (3%)
  local copies, waits for them, and re-layouts  12.9 us (3%)
    psum x2, waiting for transfers between devices, gather_panel(): summed = lax.psum(partial_panel, 'rows')  194 us
    psum x2, waiting for transfers between devices, per_device(): weights = lax.psum(partial_weights, 'cols')  88.8 us
    dot_general x2, matrix products, per_device(): jnp.dot(weights, local_basis, precision=HIGH, preferred_element_type=jnp....  39.3 us
    dot_general x2, matrix products, per_device(): jnp.dot(residual, local_basis.T, precision=HIGH, preferred_element_type=j...  30.4 us
    all_gather x2, blocking collectives, gather_panel(): return lax.all_gather(summed, 'cols', axis=1, tiled=True)  26.3 us
    gather x2, local copies, waits for them, and re-layouts, gather_panel(): taken = jnp.take(residual, local_index, axis=0)  12.8 us
    convert_element_type x1, other arithmetic, per_device(): residual = embeddings.astype(jnp.float32)  12 us
  transfers between devices with their start and end apart: 4, of which 4 were waited for; matrix products, arithmetic and copies ran while one was open for 0% of the time, Pallas kernels for 0%

commit v1 on v0

v1 whole, which is shorter than its diff:
```python
import functools

import jax
import jax.numpy as jnp
from jax import lax
from jax.experimental import pallas as pl
from jax.experimental.pallas import tpu as pltpu
from jax.sharding import PartitionSpec as P

HIGH = lax.Precision.HIGHEST
CHUNKS = 2
VMEM_LIMIT = 48 * 1024 * 1024
F32, BF16 = jnp.float32, jnp.bfloat16


def whole():
    return pl.BlockSpec(memory_space=pltpu.VMEM)


def anywhere():
    return pl.BlockSpec(memory_space=pl.ANY)


def scalars():
    return pl.BlockSpec(memory_space=pltpu.SMEM)


def in_vmem(array):
    return pltpu.with_memory_space_constraint(array, pltpu.VMEM)


def call(body, out_shape, in_specs, out_specs, scratch=(), aliases=None, name=None):
    return pl.pallas_call(
        body,
        out_shape=out_shape,
        in_specs=in_specs,
        out_specs=out_specs,
        scratch_shapes=list(scratch),
        input_output_aliases=aliases or {},
        compiler_params=pltpu.CompilerParams(vmem_limit_bytes=VMEM_LIMIT),
        name=name,
    )


def own_picks(emb, pick_rows, copies):
    rows, width = emb.shape
    rounds, picks = pick_rows.shape
    tile = 16

    def body(picks_ref, emb_ref, out_ref, held, sems):
        first = lax.axis_index("rows") * rows
        offsets, moves = [], []
        for r in range(rounds):
            local = jnp.int32(0)
            for i in range(picks):
                at = picks_ref[r, i] - first
                local = local + jnp.where((at >= 0) & (at < rows), at, 0)
            base = pl.multiple_of((local // tile) * tile, tile)
            offsets.append(local - base)
            move = pltpu.make_async_copy(emb_ref.at[pl.ds(base, tile), :], held.at[r], sems.at[r])
            move.start()
            moves.append(move)
        for r in range(rounds):
            moves[r].wait()
            block = held[r].astype(F32)
            line = lax.broadcasted_iota(jnp.int32, (tile, width), 0)
            row = jnp.sum(jnp.where(line == offsets[r], block, 0.0), axis=0, keepdims=True)
            out_ref[:, r : r + 1, :] = jnp.broadcast_to(row[None], (copies, 1, width))

    return call(
        body,
        jax.ShapeDtypeStruct((copies, rounds, width), F32),
        [scalars(), anywhere()],
        whole(),
        [pltpu.VMEM((rounds, tile, width), BF16), pltpu.SemaphoreType.DMA((rounds,))],
        name="own_picks",
    )(pick_rows, emb)


def paired_panel(panel):
    panel = panel.astype(BF16)
    zero = jnp.zeros_like(panel)
    return jnp.concatenate(
        [jnp.concatenate([panel, zero], axis=1), jnp.concatenate([zero, panel], axis=1)], axis=0
    )


def paired_products(top, bottom, paired):
    both = jnp.concatenate([top, bottom], axis=1)
    return lax.dot_general(both, paired, (((1,), (1,)), ((), ())), preferred_element_type=F32)


def diagonal_products(emb, panel, block_rows):
    picks = panel.shape[0]
    group = block_rows // (2 * CHUNKS)
    half = group // 2

    def body(emb_ref, panel_ref, gram_ref, *out_refs):
        block = lax.rem(lax.axis_index("cols") + 2, 4)
        panel = panel_ref[...]
        paired = paired_panel(panel)
        low = panel.astype(BF16)
        gram_ref[...] = paired_products(low[: picks // 2], low[picks // 2 :], paired)
        for k in range(CHUNKS):
            base = pl.multiple_of(block * block_rows + k * 2 * group, 2 * group)
            got = paired_products(emb_ref[pl.ds(base, group), :], emb_ref[pl.ds(base + group, group), :], paired)
            out_refs[2 * k][...] = got[:half]
            out_refs[2 * k + 1][...] = got[half:]

    shapes = [pltpu.VMEM((picks // 2, 2 * picks), F32)] + [pltpu.VMEM((half, 2 * picks), F32)] * (2 * CHUNKS)
    return call(body, shapes, [whole(), whole()], [whole()] * len(shapes), name="diagonal_products")(
        in_vmem(emb), in_vmem(panel)
    )


def other_products(emb, panel, block_rows):
    picks = panel.shape[0]
    group = block_rows // (2 * CHUNKS)

    def body(emb_ref, panel_ref, *out_refs):
        me = lax.axis_index("cols")
        paired = paired_panel(panel_ref[...])
        for k in range(CHUNKS):
            for j, shift in enumerate((1, 3, 0)):
                block = lax.rem(me + shift, 4)
                base = pl.multiple_of(block * block_rows + k * 2 * group, 2 * group)
                out_refs[3 * k + j][...] = paired_products(
                    emb_ref[pl.ds(base, group), :], emb_ref[pl.ds(base + group, group), :], paired
                )

    shapes = [pltpu.VMEM((group, 2 * picks), F32)] * (3 * CHUNKS)
    return call(body, shapes, [whole(), whole()], [whole()] * len(shapes), name="other_products")(
        in_vmem(emb), in_vmem(panel)
    )


def split(value):
    high = value.astype(BF16)
    rest = value - high.astype(F32)
    middle = rest.astype(BF16)
    low = (rest - middle.astype(F32)).astype(BF16)
    return high, middle, low


def dot_full(a, b):
    return jnp.dot(a, b, precision=HIGH, preferred_element_type=F32)


def update_matrix(gram_parts, panel):
    picks, width = panel.shape

    def body(*refs):
        panel_ref, out_ref = refs[-2:]
        total = refs[0][...]
        for ref in refs[1:-2]:
            total = total + ref[...]
        gram = jnp.concatenate([total[:, :picks], total[:, picks:]], axis=0)
        lane = lax.broadcasted_iota(jnp.int32, gram.shape, 1)
        line = lax.broadcasted_iota(jnp.int32, gram.shape, 0)
        inverse = gram
        for k in range(picks):
            pivot = 1.0 / inverse[k : k + 1, k : k + 1]
            row = jnp.where(lane[:1] == k, pivot, inverse[k : k + 1, :] * pivot)
            column = inverse[:, k : k + 1]
            cleared = jnp.where(lane == k, 0.0, inverse)
            inverse = jnp.where(line == k, row, cleared - column * row)
        eye = jnp.where(lane == line, 1.0, 0.0)
        inverse = inverse + dot_full(inverse, eye - dot_full(gram, inverse))
        high, middle, low = split(dot_full(inverse, panel_ref[...]))
        out_ref[...] = jnp.concatenate([high, high, high, low, middle, middle], axis=0)

    return call(
        body,
        pltpu.VMEM((6 * picks, width), BF16),
        [whole()] * (len(gram_parts) + 1),
        whole(),
        name="update_matrix",
    )(*[in_vmem(g) for g in gram_parts], in_vmem(panel))


def update(emb, right, out, pieces, block_rows, name):
    rows, width = emb.shape
    picks = right.shape[0] // 6
    group = block_rows // (2 * CHUNKS)
    step = 256
    steps = [(n, g, t) for n, (p, *_) in enumerate(pieces) for g in range(2) for t in range(0, p.shape[0], min(step, p.shape[0]))]
    step = min(step, min(p.shape[0] for p, *_ in pieces))

    def body(*refs):
        emb_ref, right_ref = refs[:2]
        packed = refs[2 : 2 + len(pieces)]
        out_ref, staged, sems = refs[-3:]
        me = lax.axis_index("cols")
        right_mat = right_ref[...]
        lane = lax.broadcasted_iota(jnp.int32, (step, 2 * picks), 1)
        moves = []
        for i, (n, g, t) in enumerate(steps):
            _, shift, k, first = pieces[n]
            block = lax.rem(me + shift, 4)
            base = pl.multiple_of(block * block_rows + k * 2 * group + g * group + first + t, step)
            got = packed[n][t : t + step, :]
            high = got.astype(BF16).astype(F32)
            rest = got - high
            middle = rest.astype(BF16).astype(F32)
            low = rest - middle
            if g == 0:
                first_part = jnp.where(lane < picks, high, pltpu.roll(middle, picks, 1))
                second_part = jnp.where(lane < picks, low, pltpu.roll(high, picks, 1))
            else:
                first_part = jnp.where(lane < picks, pltpu.roll(high, picks, 1), middle)
                second_part = jnp.where(lane < picks, pltpu.roll(low, picks, 1), high)
            first_part = first_part.astype(BF16)
            left = jnp.concatenate([first_part, second_part.astype(BF16), first_part], axis=1)
            taken = jnp.dot(left, right_mat, preferred_element_type=F32)
            staged[i] = emb_ref[pl.ds(base, step), :].astype(F32) - taken
            move = pltpu.make_async_copy(staged.at[i], out_ref.at[pl.ds(base, step), :], sems.at[i])
            move.start()
            moves.append(move)
        for move in moves:
            move.wait()

    operands = [in_vmem(emb), in_vmem(right)] + [in_vmem(p) for p, *_ in pieces]
    specs = [whole()] * len(operands)
    aliases = None
    if out is not None:
        operands.append(out)
        specs.append(anywhere())
        aliases = {len(operands) - 1: 0}
    return call(
        body,
        jax.ShapeDtypeStruct((rows, width), F32),
        specs,
        anywhere(),
        [pltpu.VMEM((len(steps), step, width), F32), pltpu.SemaphoreType.DMA((len(steps),))],
        aliases,
        name=name,
    )(*operands)


def per_device(emb, pick_rows, owners):
    rows, width = emb.shape
    rounds = pick_rows.shape[0]
    block_rows = rows // 4
    half = block_rows // (4 * CHUNKS)

    def send(value, shift):
        return lax.ppermute(value, "cols", [(i, (i + shift) % 4) for i in range(4)])

    mine = own_picks(emb, pick_rows, owners)
    panel = lax.all_to_all(mine, "rows", 0, 0, tiled=True).reshape(owners * rounds, width)
    gram, *diag = diagonal_products(emb, panel, block_rows)
    from_prev, from_next = [], []
    for k in range(CHUNKS):
        up, down = diag[2 * k], diag[2 * k + 1]
        if k == 0:
            up, down = jnp.concatenate([up, gram]), jnp.concatenate([down, gram])
        from_prev.append(send(up, 1))
        from_next.append(send(down, -1))
    others = other_products(emb, panel, block_rows)
    gram_prev, gram_next = from_prev[0][half:], from_next[0][half:]
    got_prev, got_next = [], []
    for k in range(CHUNKS):
        to_next, to_prev = others[3 * k], others[3 * k + 1]
        up = [to_next[:half] + from_prev[k][:half], to_next[half:]]
        down = [to_prev[:half], to_prev[half:] + from_next[k][:half]]
        if k == 0:
            up.append(gram_prev)
        got_prev.append(send(jnp.concatenate(up), 1))
        got_next.append(send(jnp.concatenate(down), -1))
    right = update_matrix([gram, gram_prev, gram_next, got_prev[0][2 * half :]], panel)
    own, block_prev, block_next = [], [], []
    for k in range(CHUNKS):
        total = others[3 * k + 2] + got_prev[k][: 2 * half] + got_next[k]
        own.append(total)
        block_prev.append(send(total, 1))
        block_next.append(send(total, -1))
    across_top, across_bottom = [], []
    for k in range(CHUNKS):
        across_top.append(send(block_prev[k][:half], 1))
        across_bottom.append(send(block_next[k][half:], -1))
    out = None
    for k in range(CHUNKS):
        out = update(emb, right, out, [(own[k], 0, k, 0)], block_rows, "update_own")
    for k in range(CHUNKS):
        out = update(
            emb, right, out, [(block_prev[k], 3, k, 0), (block_next[k], 1, k, 0)], block_rows, "update_near"
        )
    for k in range(CHUNKS):
        out = update(
            emb, right, out, [(across_top[k], 2, k, 0), (across_bottom[k], 2, k, half)], block_rows, "update_across"
        )
    return out


def solution(mesh):
    return jax.shard_map(
        functools.partial(per_device, owners=mesh.shape["rows"]),
        mesh=mesh,
        in_specs=(P("rows", "cols"), P()),
        out_specs=P("rows", "cols"),
        check_vma=False,
    )
```

time: 436 us -> 83.1 us (0.19)
  waiting for transfers between devices: 283 us -> 8.84 us
  matrix products: 71.4 us -> 0 us
  starting transfers between devices: 0.13 us -> 29 us
  other arithmetic: 28.4 us -> 0.27 us
  Pallas kernels: 0 us -> 21.7 us
  between operations: 13.2 us -> 0.43 us
  blocking collectives: 26.3 us -> 15 us
  local copies, waits for them, and re-layouts: 12.9 us -> 7.57 us
    psum x4 -> x0, waiting for transfers between devices: 283 us -> none  [the longest x2 194 us: gather_panel(): summed = lax.psum(partial_panel, 'rows')]
    dot_general x6 -> x0, matrix products: 70.5 us -> none  [the longest x2 39.3 us: per_device(): jnp.dot(weights, local_basis, precision=HIGH, preferred_element_type=jnp....]
    ppermute x0 -> x16, starting transfers between devices: none -> 29 us  [send(): return lax.ppermute(value, 'cols', [(i, (i + shift) % 4) for i in range(4)])]
    all_gather x2 -> x0, blocking collectives: 26.3 us -> none  [gather_panel(): return lax.all_gather(summed, 'cols', axis=1, tiled=True)]
    pallas_call x0 -> x10, Pallas kernels: none -> 21.7 us  [the longest x6 11.7 us: update(): call(body, jax.ShapeDtypeStruct((rows, width), F32), specs, anywhere(), [...]
    all_to_all x0 -> x1, blocking collectives: none -> 15 us  [per_device(): lax.all_to_all(mine, 'rows', 0, 0, tiled=True)]
    another operation x10 -> x0, other arithmetic: 13.5 us -> none  [the longest x6 7.27 us: orthonormal_panel(): factor = jnp.linalg.cholesky(gram_matrix)]
    gather x2 -> x0, local copies, waits for them, and re-layouts: 12.8 us -> none  [gather_panel(): taken = jnp.take(residual, local_index, axis=0)]
  transfers between devices with their start and end apart: 4 -> 16, of which waited for: 4 -> 5; matrix products, arithmetic and copies ran while one was open for 0% -> 0% of each run, Pallas kernels for 0% -> 22%
where the time goes in v1:
time: 83.1 us; the launch traced here: 82.8 us
  starting transfers between devices  29 us (35%)
  Pallas kernels  21.7 us (26%)
  blocking collectives  15 us (18%)
  waiting for transfers between devices  8.84 us (11%)
  local copies, waits for them, and re-layouts  7.57 us (9%)
    ppermute x16, starting transfers between devices, send(): return lax.ppermute(value, 'cols', [(i, (i + shift) % 4) for i in range(4)])  29 us
    all_to_all x1, blocking collectives, per_device(): lax.all_to_all(mine, 'rows', 0, 0, tiled=True)  15 us
    pallas_call x6, Pallas kernels, update(): call(body, jax.ShapeDtypeStruct((rows, width), F32), specs, anywhere(), [...  11.7 us
    ppermute x16, waiting for transfers between devices, send(): return lax.ppermute(value, 'cols', [(i, (i + shift) % 4) for i in range(4)])  8.84 us
    unnamed x6, local copies, waits for them, and re-layouts  7.43 us
    pallas_call x1, Pallas kernels, update_matrix(): call(body, pltpu.VMEM((6 * picks, width), BF16), [whole()] * (len(gram_pa...  6.09 us
    pallas_call x1, Pallas kernels, other_products(): call(body, shapes, [whole(), whole()], [whole()] * len(shapes), name='oth...  1.76 us
  transfers between devices with their start and end apart: 16, of which 5 were waited for; matrix products, arithmetic and copies ran while one was open for 0% of the time, Pallas kernels for 22%

profile of v1, /device:TPU:0, one launch (start us, length us, event | category | flops | bytes accessed | tf_op | source)
XLA Modules:
  0.0 82.8 jit_solution(12539071225512162765)
XLA Ops:
  0.0 0.0 copy-start.2
  0.0 0.7 copy-done.2
  0.7 1.4 %own_picks.1 = f32[32,2,512]{2,1,0:T(2,128)S(1)} custom-call(s32[2,32]{1,0:T(2,128)S(1)} %copy-done.2, bf16[8192,512]{1,0:T(8,128)(2,1)} %refs_0_.11), custom_call_target="tpu_custom_call" | custom-call | tf_op jit(solution)/shard_map/own_picks/pallas_call | solution.py:70
  2.1 15.0 %all_to_all.5 = f32[32,2,512]{2,1,0:T(2,128)S(1)} all-to-all(f32[32,2,512]{2,1,0:T(2,128)S(1)} %own_picks.1), channel_id=1, replica_groups=mesh['rows'=32,'cols'=4] {'rows'}, dimensions={0} | all-to-all | bytes 262144 | tf_op jit(solution)/shard_map/all_to_all | solution.py:250
  17.1 0.1 reshape.3.panel_ref.refs_4_
  17.2 0.0 copy-start
  17.2 3.4 %copy-done = bf16[8192,512]{1,0:T(8,128)(2,1)S(1)} copy-done((bf16[8192,512]{1,0:T(8,128)(2,1)S(1)}, bf16[8192,512]{1,0:T(8,128)(2,1)}, u32[]{:S(2)}) %copy-start) | copy-done | bytes 8388632
  20.6 0.7 diagonal_products.1
  21.3 2.0 %collective-permute-start.3 = (f32[256,128]{1,0:T(8,128)S(1)}, f32[256,128]{1,0:T(8,128)S(1)}, u32[]{:S(2)}, u32[]{:S(2)}) collective-permute-start(f32[256,128]{1,0:T(8,128)S(1)} %get-tuple-element.22), channel_id=1, source_target_pairs={{0,1},{1,2},{2,3},{3,0},{4,5},{5,6},{6,7},{7,4},{8,9},{9,10},{10,1... | collective-permute-start | bytes 393224 | tf_op jit(solution)/shard_map/ppermute | solution.py:247
  23.3 2.2 %collective-permute-start.5 = (f32[256,128]{1,0:T(8,128)S(1)}, f32[256,128]{1,0:T(8,128)S(1)}, u32[]{:S(2)}, u32[]{:S(2)}) collective-permute-start(f32[256,128]{1,0:T(8,128)S(1)} %get-tuple-element.24), channel_id=1, source_target_pairs={{0,3},{1,0},{2,1},{3,2},{4,7},{5,4},{6,5},{7,6},{8,11},{9,8},{10,9... | collective-permute-start | bytes 393224 | tf_op jit(solution)/shard_map/ppermute | solution.py:247
  25.5 1.8 %other_products.1 = (f32[512,128]{1,0:T(8,128)S(1)}, f32[512,128]{1,0:T(8,128)S(1)}, f32[512,128]{1,0:T(8,128)S(1)}, f32[512,128]{1,0:T(8,128)S(1)}, f32[512,128]{1,0:T(8,128)S(1)}, /*index=5*/f32[512,128]{1,0:T(8,128)S(1)}) custom-call(bf16[8192,512]{1,0:T(8,128)(2,1)S(1)} %copy-done, f32[64,512]{1,0:T(8,128)S(1)} %reshape.3.panel_ref.refs_4_), custom_call_target="tpu_custom_call" | custom-call | tf_op jit(solution)/shard_map/other_products/pallas_call | solution.py:132
  27.3 0.1 collective-permute-start
  27.4 3.2 %collective-permute-start.1 = (f32[288,128]{1,0:T(8,128)S(1)}, f32[288,128]{1,0:T(8,128)S(1)}, u32[]{:S(2)}, u32[]{:S(2)}) collective-permute-start(f32[288,128]{1,0:T(8,128)S(1)} %get-tuple-element.35), channel_id=1, source_target_pairs={{0,3},{1,0},{2,1},{3,2},{4,7},{5,4},{6,5},{7,6},{8,11},{9,8},{10,9... | collective-permute-start | bytes 442376 | tf_op jit(solution)/shard_map/ppermute | solution.py:247
  30.6 0.0 collective-permute-done.3
  30.6 0.0 collective-permute-done.5
  30.7 0.1 collective-permute-start.4
  30.8 3.3 %collective-permute-start.6 = (f32[512,128]{1,0:T(8,128)S(1)}, f32[512,128]{1,0:T(8,128)S(1)}, u32[]{:S(2)}, u32[]{:S(2)}) collective-permute-start(f32[512,128]{1,0:T(8,128)S(1)} %pad_maximum_fusion.2), channel_id=1, source_target_pairs={{0,3},{1,0},{2,1},{3,2},{4,7},{5,4},{6,5},{7,6},{8,11},{9,8},{10,9... | collective-permute-start | bytes 786440 | tf_op jit(solution)/shard_map/ppermute | solution.py:247
  34.1 0.3 collective-permute-done
  34.4 0.0 collective-permute-done.1
  34.5 0.4 collective-permute-start.2
  35.0 3.0 %collective-permute-start.11 = (f32[512,128]{1,0:T(8,128)S(1)}, f32[512,128]{1,0:T(8,128)S(1)}, u32[]{:S(2)}, u32[]{:S(2)}) collective-permute-start(f32[512,128]{1,0:T(8,128)S(1)} %pad_maximum_fusion.3), channel_id=1, source_target_pairs={{0,3},{1,0},{2,1},{3,2},{4,7},{5,4},{6,5},{7,6},{8,11},{9,8},{10,9... | collective-permute-start | bytes 786440 | tf_op jit(solution)/shard_map/ppermute | solution.py:247
  37.9 3.3 %collective-permute-done.4 = f32[512,128]{1,0:T(8,128)S(1)} collective-permute-done((f32[512,128]{1,0:T(8,128)S(1)}, f32[512,128]{1,0:T(8,128)S(1)}, u32[]{:S(2)}, u32[]{:S(2)}) %collective-permute-start.4) | collective-permute-done | bytes 262176 | tf_op jit(solution)/shard_map/ppermute | solution.py:247
  41.2 0.0 collective-permute-done.6
  41.3 3.4 %collective-permute-start.9 = (f32[512,128]{1,0:T(8,128)S(1)}, f32[512,128]{1,0:T(8,128)S(1)}, u32[]{:S(2)}, u32[]{:S(2)}) collective-permute-start(f32[512,128]{1,0:T(8,128)S(1)} %add_add_fusion.refs_2_), channel_id=1, source_target_pairs={{0,3},{1,0},{2,1},{3,2},{4,7},{5,4},{6,5},{7,6},{8,11},{9,8},{10,9... | collective-permute-start | bytes 786440 | tf_op jit(solution)/shard_map/ppermute | solution.py:247
  44.7 1.8 %collective-permute-done.11 = f32[512,128]{1,0:T(8,128)S(1)} collective-permute-done((f32[512,128]{1,0:T(8,128)S(1)}, f32[512,128]{1,0:T(8,128)S(1)}, u32[]{:S(2)}, u32[]{:S(2)}) %collective-permute-start.11) | collective-permute-done | bytes 262176 | tf_op jit(solution)/shard_map/ppermute | solution.py:247
  46.5 0.0 collective-permute-done.2
  46.5 0.8 collective-permute-start.12
  47.3 3.1 %collective-permute-start.14 = (f32[512,128]{1,0:T(8,128)S(1)}, f32[512,128]{1,0:T(8,128)S(1)}, u32[]{:S(2)}, u32[]{:S(2)}) collective-permute-start(f32[512,128]{1,0:T(8,128)S(1)} %fusion.refs_2_), channel_id=1, source_target_pairs={{0,3},{1,0},{2,1},{3,2},{4,7},{5,4},{6,5},{7,6},{8,11},{9,8},{10,9... | collective-permute-start | bytes 786440 | tf_op jit(solution)/shard_map/ppermute | solution.py:247
  50.4 0.0 collective-permute-start.7
  50.4 1.7 %collective-permute-done.9.refs_3_ = f32[512,128]{1,0:T(8,128)S(1)} collective-permute-done((f32[512,128]{1,0:T(8,128)S(1)}, f32[512,128]{1,0:T(8,128)S(1)}, u32[]{:S(2)}, u32[]{:S(2)}) %collective-permute-start.9) | collective-permute-done | bytes 262176 | tf_op jit(solution)/shard_map/ppermute | solution.py:247
  52.1 3.8 %collective-permute-start.10 = (f32[256,128]{1,0:T(8,128)S(1)}, f32[256,128]{1,0:T(8,128)S(1)}, u32[]{:S(2)}, u32[]{:S(2)}) collective-permute-start(f32[256,128]{1,0:T(8,128)S(1)} %slice.77), channel_id=1, source_target_pairs={{0,3},{1,0},{2,1},{3,2},{4,7},{5,4},{6,5},{7,6},{8,11},{9,8},{10,9... | collective-permute-start | bytes 393224 | tf_op jit(solution)/shard_map/ppermute | solution.py:247
  55.9 1.6 %collective-permute-done.12.refs_2_ = f32[512,128]{1,0:T(8,128)S(1)} collective-permute-done((f32[512,128]{1,0:T(8,128)S(1)}, f32[512,128]{1,0:T(8,128)S(1)}, u32[]{:S(2)}, u32[]{:S(2)}) %collective-permute-start.12) | collective-permute-done | bytes 262176 | tf_op jit(solution)/shard_map/ppermute | solution.py:247
  57.5 0.1 collective-permute-start.13
  57.6 0.0 collective-permute-done.14.refs_3_
  57.7 3.4 %collective-permute-start.15 = (f32[256,128]{1,0:T(8,128)S(1)}, f32[256,128]{1,0:T(8,128)S(1)}, u32[]{:S(2)}, u32[]{:S(2)}) collective-permute-start(f32[256,128]{1,0:T(8,128)S(1)} %slice.81), channel_id=1, source_target_pairs={{0,3},{1,0},{2,1},{3,2},{4,7},{5,4},{6,5},{7,6},{8,11},{9,8},{10,9... | collective-permute-start | bytes 393224 | tf_op jit(solution)/shard_map/ppermute | solution.py:247
  61.1 0.0 collective-permute-done.7.refs_2_
  61.1 0.3 collective-permute-start.8
  61.4 6.1 %update_matrix.1.refs_1_ = bf16[384,512]{1,0:T(8,128)(2,1)S(1)} custom-call(f32[32,128]{1,0:T(8,128)S(1)} %get-tuple-element.16.refs_0_, f32[32,128]{1,0:T(8,128)S(1)} %slice.72.refs_1_, f32[32,128]{1,0:T(8,128)S(1)} %slice.73.refs_2_, f32[32,128]{1,0:T(8,128)S(1)} %slice.75.refs_3_, f32[64,512]{1,0:T(8,128)S(1)} %reshape.3.panel_ref.refs_4_), custom_call_target="tpu_custom_call" | custom-call | tf_op jit(solution)/shard_map/update_matrix/pallas_call | solution.py:172
  67.5 0.0 copy-start.1
  67.5 3.4 %copy-done.1 = bf16[8192,512]{1,0:T(8,128)(2,1)S(1)} copy-done((bf16[8192,512]{1,0:T(8,128)(2,1)S(1)}, bf16[8192,512]{1,0:T(8,128)(2,1)}, u32[]{:S(2)}) %copy-start.1) | copy-done | bytes 8388632
  70.9 1.7 %update_own.2.refs_3_ = f32[8192,512]{1,0:T(8,128)} custom-call(bf16[8192,512]{1,0:T(8,128)(2,1)S(1)} %copy-done.1, bf16[384,512]{1,0:T(8,128)(2,1)S(1)} %update_matrix.1.refs_1_, f32[512,128]{1,0:T(8,128)S(1)} %fusion.refs_2_), custom_call_target="tpu_custom_call" | custom-call | tf_op jit(solution)/shard_map/update_own/pallas_call | solution.py:229
  72.6 1.7 %update_own.3.refs_4_ = f32[8192,512]{1,0:T(8,128)} custom-call(bf16[8192,512]{1,0:T(8,128)(2,1)S(1)} %copy-done.1, bf16[384,512]{1,0:T(8,128)(2,1)S(1)} %update_matrix.1.refs_1_, f32[512,128]{1,0:T(8,128)S(1)} %add_add_fusion.refs_2_, f32[8192,512]{1,0:T(8,128)} %update_own.2.refs_3_), custom_call_target="tpu_custom_call", output_to_operand_aliasing={{}: (3, {})} | custom-call | tf_op jit(solution)/shard_map/update_own/pallas_call | solution.py:229
  74.3 2.4 %update_near.2.refs_4_ = f32[8192,512]{1,0:T(8,128)} custom-call(bf16[8192,512]{1,0:T(8,128)(2,1)S(1)} %copy-done.1, bf16[384,512]{1,0:T(8,128)(2,1)S(1)} %update_matrix.1.refs_1_, f32[512,128]{1,0:T(8,128)S(1)} %collective-permute-done.12.refs_2_, f32[512,128]{1,0:T(8,128)S(1)} %collective-permute-done.14.refs_3_, ...), custom_call_target="tpu_custom_call", output_to_operand_aliasing={{}: (4, {})} | custom-call | tf_op jit(solution)/shard_map/update_near/pallas_call | solution.py:229
  76.7 2.4 %update_near.3.refs_4_ = f32[8192,512]{1,0:T(8,128)} custom-call(bf16[8192,512]{1,0:T(8,128)(2,1)S(1)} %copy-done.1, bf16[384,512]{1,0:T(8,128)(2,1)S(1)} %update_matrix.1.refs_1_, f32[512,128]{1,0:T(8,128)S(1)} %collective-permute-done.7.refs_2_, f32[512,128]{1,0:T(8,128)S(1)} %collective-permute-done.9.refs_3_, ...), custom_call_target="tpu_custom_call", output_to_operand_aliasing={{}: (4, {})} | custom-call | tf_op jit(solution)/shard_map/update_near/pallas_call | solution.py:229
  79.2 0.0 collective-permute-done.13.refs_2_
  79.2 0.0 collective-permute-done.15.refs_3_
  79.2 1.7 %update_across.2.refs_4_ = f32[8192,512]{1,0:T(8,128)} custom-call(bf16[8192,512]{1,0:T(8,128)(2,1)S(1)} %copy-done.1, bf16[384,512]{1,0:T(8,128)(2,1)S(1)} %update_matrix.1.refs_1_, f32[256,128]{1,0:T(8,128)S(1)} %collective-permute-done.13.refs_2_, f32[256,128]{1,0:T(8,128)S(1)} %collective-permute-done.15.refs_3_, ...), custom_call_target="tpu_custom_call", output_to_operand_aliasing={{}: (4, {})} | custom-call | tf_op jit(solution)/shard_map/update_across/pallas_call | solution.py:229
  80.9 0.0 collective-permute-done.10.refs_3_
  80.9 0.0 collective-permute-done.8.refs_2_
  80.9 1.7 %update_across.3 = f32[8192,512]{1,0:T(8,128)} custom-call(bf16[8192,512]{1,0:T(8,128)(2,1)S(1)} %copy-done.1, bf16[384,512]{1,0:T(8,128)(2,1)S(1)} %update_matrix.1.refs_1_, f32[256,128]{1,0:T(8,128)S(1)} %collective-permute-done.8.refs_2_, f32[256,128]{1,0:T(8,128)S(1)} %collective-permute-done.10.refs_3_, ...), custom_call_target="tpu_custom_call", output_to_operand_aliasing={{}: (4, {})} | custom-call | tf_op jit(solution)/shard_map/update_across/pallas_call | solution.py:229
  (16 shorter events, 0.3 us)
Async XLA Ops:
  0.0 0.7 copy-start.2
  17.2 3.4 %copy-start = (bf16[8192,512]{1,0:T(8,128)(2,1)S(1)}, bf16[8192,512]{1,0:T(8,128)(2,1)}, u32[]{:S(2)}) copy-start(bf16[8192,512]{1,0:T(8,128)(2,1)} %refs_0_.11) | copy-start | bytes 25165828
  21.3 9.3 %collective-permute-start.3 = (f32[256,128]{1,0:T(8,128)S(1)}, f32[256,128]{1,0:T(8,128)S(1)}, u32[]{:S(2)}, u32[]{:S(2)}) collective-permute-start(f32[256,128]{1,0:T(8,128)S(1)} %get-tuple-element.22), channel_id=1, source_target_pairs={{0,1},{1,2},{2,3},{3,0},{4,5},{5,6},{6,7},{7,4},{8,9},{9,10},{10,1... | collective-permute-start | bytes 393224 | tf_op jit(solution)/shard_map/ppermute | solution.py:247
  23.3 7.3 %collective-permute-start.5 = (f32[256,128]{1,0:T(8,128)S(1)}, f32[256,128]{1,0:T(8,128)S(1)}, u32[]{:S(2)}, u32[]{:S(2)}) collective-permute-start(f32[256,128]{1,0:T(8,128)S(1)} %get-tuple-element.24), channel_id=1, source_target_pairs={{0,3},{1,0},{2,1},{3,2},{4,7},{5,4},{6,5},{7,6},{8,11},{9,8},{10,9... | collective-permute-start | bytes 393224 | tf_op jit(solution)/shard_map/ppermute | solution.py:247
  27.3 7.1 %collective-permute-start = (f32[288,128]{1,0:T(8,128)S(1)}, f32[288,128]{1,0:T(8,128)S(1)}, u32[]{:S(2)}, u32[]{:S(2)}) collective-permute-start(f32[288,128]{1,0:T(8,128)S(1)} %get-tuple-element.36), channel_id=1, source_target_pairs={{0,1},{1,2},{2,3},{3,0},{4,5},{5,6},{6,7},{7,4},{8,9},{9,10},{10,1... | collective-permute-start | bytes 442376 | tf_op jit(solution)/shard_map/ppermute | solution.py:247
  27.4 7.0 %collective-permute-start.1 = (f32[288,128]{1,0:T(8,128)S(1)}, f32[288,128]{1,0:T(8,128)S(1)}, u32[]{:S(2)}, u32[]{:S(2)}) collective-permute-start(f32[288,128]{1,0:T(8,128)S(1)} %get-tuple-element.35), channel_id=1, source_target_pairs={{0,3},{1,0},{2,1},{3,2},{4,7},{5,4},{6,5},{7,6},{8,11},{9,8},{10,9... | collective-permute-start | bytes 442376 | tf_op jit(solution)/shard_map/ppermute | solution.py:247
  30.7 10.5 %collective-permute-start.4 = (f32[512,128]{1,0:T(8,128)S(1)}, f32[512,128]{1,0:T(8,128)S(1)}, u32[]{:S(2)}, u32[]{:S(2)}) collective-permute-start(f32[512,128]{1,0:T(8,128)S(1)} %pad_maximum_fusion.1), channel_id=1, source_target_pairs={{0,1},{1,2},{2,3},{3,0},{4,5},{5,6},{6,7},{7,4},{8,9},{9,10},{10,1... | collective-permute-start | bytes 786440 | tf_op jit(solution)/shard_map/ppermute | solution.py:247
  30.8 10.4 %collective-permute-start.6 = (f32[512,128]{1,0:T(8,128)S(1)}, f32[512,128]{1,0:T(8,128)S(1)}, u32[]{:S(2)}, u32[]{:S(2)}) collective-permute-start(f32[512,128]{1,0:T(8,128)S(1)} %pad_maximum_fusion.2), channel_id=1, source_target_pairs={{0,3},{1,0},{2,1},{3,2},{4,7},{5,4},{6,5},{7,6},{8,11},{9,8},{10,9... | collective-permute-start | bytes 786440 | tf_op jit(solution)/shard_map/ppermute | solution.py:247
  34.5 12.0 %collective-permute-start.2 = (f32[544,128]{1,0:T(8,128)S(1)}, f32[544,128]{1,0:T(8,128)S(1)}, u32[]{:S(2)}, u32[]{:S(2)}) collective-permute-start(f32[544,128]{1,0:T(8,128)S(1)} %pad_maximum_fusion), channel_id=1, source_target_pairs={{0,1},{1,2},{2,3},{3,0},{4,5},{5,6},{6,7},{7,4},{8,9},{9,10},{10,1... | collective-permute-start | bytes 835592 | tf_op jit(solution)/shard_map/ppermute | solution.py:247
  35.0 11.5 %collective-permute-start.11 = (f32[512,128]{1,0:T(8,128)S(1)}, f32[512,128]{1,0:T(8,128)S(1)}, u32[]{:S(2)}, u32[]{:S(2)}) collective-permute-start(f32[512,128]{1,0:T(8,128)S(1)} %pad_maximum_fusion.3), channel_id=1, source_target_pairs={{0,3},{1,0},{2,1},{3,2},{4,7},{5,4},{6,5},{7,6},{8,11},{9,8},{10,9... | collective-permute-start | bytes 786440 | tf_op jit(solution)/shard_map/ppermute | solution.py:247
  41.3 10.8 %collective-permute-start.9 = (f32[512,128]{1,0:T(8,128)S(1)}, f32[512,128]{1,0:T(8,128)S(1)}, u32[]{:S(2)}, u32[]{:S(2)}) collective-permute-start(f32[512,128]{1,0:T(8,128)S(1)} %add_add_fusion.refs_2_), channel_id=1, source_target_pairs={{0,3},{1,0},{2,1},{3,2},{4,7},{5,4},{6,5},{7,6},{8,11},{9,8},{10,9... | collective-permute-start | bytes 786440 | tf_op jit(solution)/shard_map/ppermute | solution.py:247
  46.5 11.0 %collective-permute-start.12 = (f32[512,128]{1,0:T(8,128)S(1)}, f32[512,128]{1,0:T(8,128)S(1)}, u32[]{:S(2)}, u32[]{:S(2)}) collective-permute-start(f32[512,128]{1,0:T(8,128)S(1)} %fusion.refs_2_), channel_id=1, source_target_pairs={{0,1},{1,2},{2,3},{3,0},{4,5},{5,6},{6,7},{7,4},{8,9},{9,10},{10,1... | collective-permute-start | bytes 786440 | tf_op jit(solution)/shard_map/ppermute | solution.py:247
  47.3 10.3 %collective-permute-start.14 = (f32[512,128]{1,0:T(8,128)S(1)}, f32[512,128]{1,0:T(8,128)S(1)}, u32[]{:S(2)}, u32[]{:S(2)}) collective-permute-start(f32[512,128]{1,0:T(8,128)S(1)} %fusion.refs_2_), channel_id=1, source_target_pairs={{0,3},{1,0},{2,1},{3,2},{4,7},{5,4},{6,5},{7,6},{8,11},{9,8},{10,9... | collective-permute-start | bytes 786440 | tf_op jit(solution)/shard_map/ppermute | solution.py:247
  50.4 10.7 %collective-permute-start.7 = (f32[512,128]{1,0:T(8,128)S(1)}, f32[512,128]{1,0:T(8,128)S(1)}, u32[]{:S(2)}, u32[]{:S(2)}) collective-permute-start(f32[512,128]{1,0:T(8,128)S(1)} %add_add_fusion.refs_2_), channel_id=1, source_target_pairs={{0,1},{1,2},{2,3},{3,0},{4,5},{5,6},{6,7},{7,4},{8,9},{9,10},{10,1... | collective-permute-start | bytes 786440 | tf_op jit(solution)/shard_map/ppermute | solution.py:247
  52.1 28.8 %collective-permute-start.10 = (f32[256,128]{1,0:T(8,128)S(1)}, f32[256,128]{1,0:T(8,128)S(1)}, u32[]{:S(2)}, u32[]{:S(2)}) collective-permute-start(f32[256,128]{1,0:T(8,128)S(1)} %slice.77), channel_id=1, source_target_pairs={{0,3},{1,0},{2,1},{3,2},{4,7},{5,4},{6,5},{7,6},{8,11},{9,8},{10,9... | collective-permute-start | bytes 393224 | tf_op jit(solution)/shard_map/ppermute | solution.py:247
  57.5 21.6 %collective-permute-start.13 = (f32[256,128]{1,0:T(8,128)S(1)}, f32[256,128]{1,0:T(8,128)S(1)}, u32[]{:S(2)}, u32[]{:S(2)}) collective-permute-start(f32[256,128]{1,0:T(8,128)S(1)} %slice.80), channel_id=1, source_target_pairs={{0,1},{1,2},{2,3},{3,0},{4,5},{5,6},{6,7},{7,4},{8,9},{9,10},{10,1... | collective-permute-start | bytes 393224 | tf_op jit(solution)/shard_map/ppermute | solution.py:247
  57.7 21.5 %collective-permute-start.15 = (f32[256,128]{1,0:T(8,128)S(1)}, f32[256,128]{1,0:T(8,128)S(1)}, u32[]{:S(2)}, u32[]{:S(2)}) collective-permute-start(f32[256,128]{1,0:T(8,128)S(1)} %slice.81), channel_id=1, source_target_pairs={{0,3},{1,0},{2,1},{3,2},{4,7},{5,4},{6,5},{7,6},{8,11},{9,8},{10,9... | collective-permute-start | bytes 393224 | tf_op jit(solution)/shard_map/ppermute | solution.py:247
  61.1 19.8 %collective-permute-start.8 = (f32[256,128]{1,0:T(8,128)S(1)}, f32[256,128]{1,0:T(8,128)S(1)}, u32[]{:S(2)}, u32[]{:S(2)}) collective-permute-start(f32[256,128]{1,0:T(8,128)S(1)} %slice.76), channel_id=1, source_target_pairs={{0,1},{1,2},{2,3},{3,0},{4,5},{5,6},{6,7},{7,4},{8,9},{9,10},{10,1... | collective-permute-start | bytes 393224 | tf_op jit(solution)/shard_map/ppermute | solution.py:247
  67.5 3.4 %copy-start.1 = (bf16[8192,512]{1,0:T(8,128)(2,1)S(1)}, bf16[8192,512]{1,0:T(8,128)(2,1)}, u32[]{:S(2)}) copy-start(bf16[8192,512]{1,0:T(8,128)(2,1)} %refs_0_.11) | copy-start | bytes 25165828

commit v2 on v1

v2 whole, which is shorter than its diff:
```python
import functools

import jax
import jax.numpy as jnp
from jax import lax
from jax.experimental import pallas as pl
from jax.experimental.pallas import tpu as pltpu
from jax.sharding import PartitionSpec as P

HIGH = lax.Precision.HIGHEST
CHUNKS = (512, 512)
VMEM_LIMIT = 16 * 1024 * 1024
F32, BF16 = jnp.float32, jnp.bfloat16


def whole():
    return pl.BlockSpec(memory_space=pltpu.VMEM)


def anywhere():
    return pl.BlockSpec(memory_space=pl.ANY)


def scalars():
    return pl.BlockSpec(memory_space=pltpu.SMEM)


def in_vmem(array):
    return pltpu.with_memory_space_constraint(array, pltpu.VMEM)


def in_hbm(array):
    return pltpu.with_memory_space_constraint(array, pltpu.HBM)


def in_hbm(array):
    return pltpu.with_memory_space_constraint(array, pltpu.HBM)


def call(body, out_shape, in_specs, out_specs, scratch=(), aliases=None, name=None, micros=1.0):
    return pl.pallas_call(
        body,
        out_shape=out_shape,
        in_specs=in_specs,
        out_specs=out_specs,
        scratch_shapes=list(scratch),
        input_output_aliases=aliases or {},
        compiler_params=pltpu.CompilerParams(vmem_limit_bytes=VMEM_LIMIT),
        cost_estimate=pl.CostEstimate(flops=0, bytes_accessed=int(micros * 3.0e6), transcendentals=0),
        name=name,
    )


def first_partner(core, place):
    return place ^ 1 if core == 0 else place ^ 3


def second_partner(core, place):
    return place ^ 3 if core == 0 else place ^ 1


def kept():
    place, odd = lax.axis_index("cols"), lax.rem(lax.axis_index("rows"), 2) == 1
    high, low = place // 2, lax.rem(place, 2)
    gray = lax.rem(high + low, 2)
    return jnp.where(odd, high, gray), jnp.where(odd, low, high), jnp.where(odd, 1 - low, high)


def tile_of(size):
    return max(s for s in range(16, 257, 16) if size % s == 0)


def block_start(half, quarter, block_rows, chunk):
    return (2 * half + quarter) * block_rows + 2 * sum(CHUNKS[:chunk])


def own_picks(emb, pick_rows, copies, block_rows):
    rows, width = emb.shape
    rounds, picks = pick_rows.shape
    tile, size = 16, 2 * CHUNKS[0]

    def body(picks_ref, emb_ref, out_ref, ahead_ref, table, held, sems, table_sem, ahead_sems):
        load = pltpu.make_async_copy(picks_ref, table, table_sem)
        load.start()
        half, _, quarter = kept()
        moves = []
        for j in range(2):
            base = block_start(1 - half, quarter if j else 1 - quarter, block_rows, 0)
            for g in range(2):
                at = g * (size // 2)
                moves.append(
                    pltpu.make_async_copy(
                        emb_ref.at[pl.ds(pl.multiple_of(base + at, 16), size // 2), :],
                        ahead_ref.at[j, pl.ds(at, size // 2), :],
                        ahead_sems.at[2 * j + g],
                    )
                )
        load.wait()
        first = lax.axis_index("rows") * rows
        offsets, found = [], []
        for r in range(rounds):
            local = jnp.int32(0)
            for i in range(picks):
                at = table[r, i] - first
                local = local + jnp.where((at >= 0) & (at < rows), at, 0)
            base = pl.multiple_of((local // tile) * tile, tile)
            offsets.append(local - base)
            move = pltpu.make_async_copy(emb_ref.at[pl.ds(base, tile), :], held.at[r], sems.at[r])
            move.start()
            found.append(move)
        for move in moves:
            move.start()
        for r in range(rounds):
            found[r].wait()
            block = held[r].astype(F32)
            line = lax.broadcasted_iota(jnp.int32, (tile, width), 0)
            row = jnp.sum(jnp.where(line == offsets[r], block, 0.0), axis=0, keepdims=True)
            out_ref[:, r : r + 1, :] = jnp.broadcast_to(row[None], (copies, 1, width))
        for move in moves:
            move.wait()

    return call(
        body,
        [pltpu.VMEM((copies, rounds, width), F32), pltpu.VMEM((2, size, width), BF16)],
        [anywhere(), anywhere()],
        [whole(), whole()],
        [
            pltpu.SMEM((rounds, picks), jnp.int32),
            pltpu.VMEM((rounds, tile, width), BF16),
            pltpu.SemaphoreType.DMA((rounds,)),
            pltpu.SemaphoreType.DMA,
            pltpu.SemaphoreType.DMA((4,)),
        ],
        name="own_picks",
    )(in_hbm(pick_rows), in_hbm(emb))


def paired_panel(panel):
    panel = panel.astype(BF16)
    zero = jnp.zeros_like(panel)
    return jnp.concatenate(
        [jnp.concatenate([panel, zero], axis=1), jnp.concatenate([zero, panel], axis=1)], axis=0
    )


def paired_products(top, bottom, paired):
    both = jnp.concatenate([top, bottom], axis=1)
    return lax.dot_general(both, paired, (((1,), (1,)), ((), ())), preferred_element_type=F32)


def given_first(ahead, panel):
    picks = panel.shape[0]
    size = CHUNKS[0]

    def body(ahead_ref, panel_ref, out_ref):
        panel = panel_ref[...]
        paired = paired_panel(panel)
        low = panel.astype(BF16)
        out_ref[2 * size :, :] = paired_products(low[: picks // 2], low[picks // 2 :], paired)
        for j in range(2):
            out_ref[j * size : (j + 1) * size, :] = paired_products(ahead_ref[j, :size, :], ahead_ref[j, size:, :], paired)

    return call(
        body, pltpu.VMEM((2 * size + picks // 2, 2 * picks), F32), [whole(), whole()], whole(), name="given_first"
    )(in_vmem(ahead), in_vmem(panel))


def quarter_products(emb_ref, start, size, paired):
    start = pl.multiple_of(start, 16)
    return paired_products(emb_ref[pl.ds(start, size), :], emb_ref[pl.ds(start + size, size), :], paired)


def given_rest(emb, panel, block_rows, chunks, after):
    picks = panel.shape[0]

    def body(emb_ref, panel_ref, _, *out_refs):
        half, _, quarter = kept()
        paired = paired_panel(panel_ref[...])
        for out_ref, k in zip(out_refs, chunks):
            size = CHUNKS[k]
            for j in range(2):
                start = block_start(1 - half, quarter if j else 1 - quarter, block_rows, k)
                out_ref[j * size : (j + 1) * size, :] = quarter_products(emb_ref, start, size, paired)

    shapes = [pltpu.VMEM((2 * CHUNKS[k], 2 * picks), F32) for k in chunks]
    return call(body, shapes, [whole(), whole(), anywhere()], [whole()] * len(shapes), name="given_rest")(
        emb, in_vmem(panel), after
    )


def kept_products(emb, panel, got, message, block_rows, k):
    picks = panel.shape[0]
    size = CHUNKS[k]
    extra = picks // 2 if k == 0 else 0

    def body(emb_ref, panel_ref, got_ref, mine_ref, out_ref, own_ref):
        half, quarter, _ = kept()
        paired = paired_panel(panel_ref[...])
        start = block_start(half, 1 - quarter, block_rows, k)
        out_ref[:size, :] = quarter_products(emb_ref, start, size, paired) + got_ref[:size, :]
        if extra:
            out_ref[size:, :] = got_ref[2 * size :, :] + mine_ref[2 * size :, :]
        start = block_start(half, quarter, block_rows, k)
        own_ref[...] = quarter_products(emb_ref, start, size, paired) + got_ref[size : 2 * size, :]

    return call(
        body,
        [pltpu.VMEM((size + extra, 2 * picks), F32), pltpu.VMEM((size, 2 * picks), F32)],
        [whole()] * 4,
        [whole()] * 2,
        name="kept_products",
    )(emb, in_vmem(panel), in_vmem(got), in_vmem(message))


def added(own, got, after):
    def body(own_ref, got_ref, *refs):
        refs[-1][...] = own_ref[...] + got_ref[: own.shape[0], :]

    return call(
        body, pltpu.VMEM(own.shape, F32), [whole(), whole()] + [anywhere()] * len(after), whole(), name="added"
    )(in_vmem(own), in_vmem(got), *after)


def stacked(top, bottom, after):
    def body(top_ref, bottom_ref, *refs):
        refs[-1][: top.shape[0], :] = top_ref[...]
        refs[-1][top.shape[0] :, :] = bottom_ref[...]

    return call(
        body,
        pltpu.VMEM((top.shape[0] + bottom.shape[0], top.shape[1]), F32),
        [whole(), whole()] + [anywhere()] * len(after),
        whole(),
        name="stacked",
    )(in_vmem(top), in_vmem(bottom), *after)


def split(value):
    high = value.astype(BF16)
    rest = value - high.astype(F32)
    middle = rest.astype(BF16)
    low = (rest - middle.astype(F32)).astype(BF16)
    return high, middle, low


def dot_full(a, b):
    return jnp.dot(a, b, precision=HIGH, preferred_element_type=F32)


def gram_of(sent_ref, got_ref):
    total = sent_ref[CHUNKS[0] :, :] + got_ref[CHUNKS[0] :, :]
    picks = total.shape[1] // 2
    return jnp.concatenate([total[:, :picks], total[:, picks:]], axis=0)


def inverted(matrix):
    lane = lax.broadcasted_iota(jnp.int32, matrix.shape, 1)
    line = lax.broadcasted_iota(jnp.int32, matrix.shape, 0)
    for k in range(0, matrix.shape[0], 2):
        first = jnp.broadcast_to(matrix[:, k : k + 1], matrix.shape)
        second = jnp.broadcast_to(matrix[:, k + 1 : k + 2], matrix.shape)
        a, b, d = first[k : k + 1], second[k : k + 1], second[k + 1 : k + 2]
        scale = 1.0 / (a * d - b * b)
        here, there = lane[:1] == k, lane[:1] == k + 1
        top = jnp.where(here, 1.0, jnp.where(there, 0.0, matrix[k : k + 1]))
        bottom = jnp.where(there, 1.0, jnp.where(here, 0.0, matrix[k + 1 : k + 2]))
        row = (d * top - b * bottom) * scale
        next_row = (a * bottom - b * top) * scale
        cleared = jnp.where((lane == k) | (lane == k + 1), 0.0, matrix)
        rest = cleared - first * row - second * next_row
        matrix = jnp.where(line == k, row, jnp.where(line == k + 1, next_row, rest))
    return matrix


def update_matrix(sent, got, panel):
    picks, width = panel.shape

    def body(sent_ref, got_ref, panel_ref, out_ref):
        gram = gram_of(sent_ref, got_ref)
        inverse = inverted(gram)
        lane = lax.broadcasted_iota(jnp.int32, gram.shape, 1)
        line = lax.broadcasted_iota(jnp.int32, gram.shape, 0)
        eye = jnp.where(lane == line, 1.0, 0.0)
        inverse = inverse + dot_full(inverse, eye - dot_full(gram, inverse))
        high, middle, low = split(dot_full(inverse, panel_ref[...]))
        out_ref[...] = jnp.concatenate([high, high, high, low, middle, middle], axis=0)

    return call(body, pltpu.VMEM((6 * picks, width), BF16), [whole()] * 3, whole(), name="update_matrix")(
        in_vmem(sent), in_vmem(got), in_vmem(panel)
    )


def update(emb, right, out, pieces, block_rows, name):
    rows, width = emb.shape
    picks = right.shape[0] // 6
    steps = []
    for n, (_, _, k, *_) in enumerate(pieces):
        size = CHUNKS[k]
        step = tile_of(size)
        steps += [(n, g, t, step) for g in range(2) for t in range(0, size, step)]
    biggest = max(s[3] for s in steps)
    count = len(pieces)

    def body(*refs):
        emb_ref, right_ref = refs[:2]
        out_ref, staged, sems = refs[-3:]
        half, quarter, partner_quarter = kept()
        right_mat = right_ref[...]
        moves = []
        for i, (n, g, t, step) in enumerate(steps):
            _, first, k, give, keeper = pieces[n]
            size = CHUNKS[k]
            own_half, own_quarter = (1 - half, partner_quarter) if give else (half, quarter)
            start = block_start(own_half, own_quarter if keeper else 1 - own_quarter, block_rows, k)
            base = pl.multiple_of(start + g * size + t, 16)
            got = refs[2 + n][first + t : first + t + step, :]
            lane = lax.broadcasted_iota(jnp.int32, (step, 2 * picks), 1)
            high = got.astype(BF16).astype(F32)
            rest = got - high
            middle = rest.astype(BF16).astype(F32)
            low = rest - middle
            if g == 0:
                first_part = jnp.where(lane < picks, high, pltpu.roll(middle, picks, 1))
                second_part = jnp.where(lane < picks, low, pltpu.roll(high, picks, 1))
            else:
                first_part = jnp.where(lane < picks, pltpu.roll(high, picks, 1), middle)
                second_part = jnp.where(lane < picks, pltpu.roll(low, picks, 1), high)
            first_part = first_part.astype(BF16)
            left = jnp.concatenate([first_part, second_part.astype(BF16), first_part], axis=1)
            taken = jnp.dot(left, right_mat, preferred_element_type=F32)
            staged[i, :step] = emb_ref[pl.ds(base, step), :].astype(F32) - taken
            move = pltpu.make_async_copy(staged.at[i, pl.ds(0, step)], out_ref.at[pl.ds(base, step), :], sems.at[i])
            move.start()
            moves.append(move)
        for move in moves:
            move.wait()

    operands = [emb, in_vmem(right)] + [in_vmem(p[0]) for p in pieces]
    specs = [whole()] * len(operands)
    aliases = None
    if out is not None:
        operands.append(out)
        specs.append(anywhere())
        aliases = {len(operands) - 1: 0}
    return call(
        body,
        jax.ShapeDtypeStruct((rows, width), F32),
        specs,
        anywhere(),
        [pltpu.VMEM((len(steps), biggest, width), F32), pltpu.SemaphoreType.DMA((len(steps),))],
        aliases,
        name=name,
    )(*operands)


def per_device(emb, pick_rows, owners):
    rows, width = emb.shape
    rounds = pick_rows.shape[0]
    block_rows = rows // 4
    count = len(CHUNKS)
    first_pairs = [(r * 4 + c, r * 4 + first_partner(r % 2, c)) for r in range(owners) for c in range(4)]
    second_pairs = [(r * 4 + c, r * 4 + second_partner(r % 2, c)) for r in range(owners) for c in range(4)]

    def swap_first(value):
        return lax.ppermute(value, ("rows", "cols"), first_pairs)

    def swap_second(value):
        return lax.ppermute(value, ("rows", "cols"), second_pairs)

    mine, ahead = own_picks(emb, pick_rows, owners, block_rows)
    panel = lax.all_to_all(mine, "rows", 0, 0, tiled=True).reshape(owners * rounds, width)

    messages = [given_first(ahead, panel)]
    messages += given_rest(emb, panel, block_rows, list(range(1, count)), messages[0])
    halves = [swap_first(m) for m in messages]
    sent, own = zip(*[kept_products(emb, panel, halves[k], messages[k], block_rows, k) for k in range(count)])
    quarters = [swap_second(m) for m in sent]
    right = update_matrix(sent[0], quarters[0], panel)

    totals, near, far = [], [], []
    for k in range(count):
        totals.append(added(own[k], quarters[k], [right] if k else []))
        near.append(swap_second(totals[k]))
    for k in range(count):
        far.append((swap_first(totals[k]), swap_first(near[k])))
    out = None
    for k in range(count):
        out = update(emb, right, out, [(totals[k], 0, k, False, True), (near[k], 0, k, False, False)], block_rows, "update_near")
    for k in range(count):
        pieces = [(far[k][0], 0, k, True, True), (far[k][1], 0, k, True, False)]
        out = update(emb, right, out, pieces, block_rows, "update_far")
    return out


def solution(mesh):
    return jax.shard_map(
        functools.partial(per_device, owners=mesh.shape["rows"]),
        mesh=mesh,
        in_specs=(P("rows", "cols"), P()),
        out_specs=P("rows", "cols"),
        check_vma=False,
    )
```

time: 83.1 us -> 65.7 us (0.79)
  starting transfers between devices: 29 us -> 16.4 us
  local copies, waits for them, and re-layouts: 7.57 us -> 3.48 us
  Pallas kernels: 21.7 us -> 18.6 us
  waiting for transfers between devices: 8.84 us -> 11.3 us
    ppermute x16 -> x10, starting transfers between devices: 29 us -> 16.4 us  [the longest x4 12.2 us: swap_second(): return lax.ppermute(value, ('rows', 'cols'), second_pairs)]
    unnamed x6, local copies, waits for them, and re-layouts: 7.43 us -> 3.39 us
    ppermute x16 -> x10, waiting for transfers between devices: 8.84 us -> 11.3 us  [the longest x6 6.17 us: swap_first(): return lax.ppermute(value, ('rows', 'cols'), first_pairs)]
    pallas_call x6 -> x4, Pallas kernels: 11.7 us -> 9.71 us  [update(): call(body, jax.ShapeDtypeStruct((rows, width), F32), specs, anywhere(), [...]
    pallas_call x4 -> x8, Pallas kernels: 10 us -> 8.85 us  [the longest x1 3.7 us: update_matrix(): call(body, pltpu.VMEM((6 * picks, width), BF16), [whole()] * 3, whole(),...]
  transfers between devices with their start and end apart: 16 -> 10, of which waited for: 5 -> 4; matrix products, arithmetic and copies ran while one was open for 0% -> 0% of each run, Pallas kernels for 22% -> 20%
where the time goes in v2:
time: 65.7 us; the launch traced here: 65 us
  Pallas kernels  18.6 us (28%)
  starting transfers between devices  16.4 us (25%)
  blocking collectives  15 us (23%)
  waiting for transfers between devices  11.3 us (17%)
  local copies, waits for them, and re-layouts  3.48 us (5%)
    all_to_all x1, blocking collectives, per_device(): lax.all_to_all(mine, 'rows', 0, 0, tiled=True)  15 us
    ppermute x4, starting transfers between devices, swap_second(): return lax.ppermute(value, ('rows', 'cols'), second_pairs)  12.2 us
    pallas_call x4, Pallas kernels, update(): call(body, jax.ShapeDtypeStruct((rows, width), F32), specs, anywhere(), [...  9.71 us
    ppermute x6, waiting for transfers between devices, swap_first(): return lax.ppermute(value, ('rows', 'cols'), first_pairs)  6.17 us
    ppermute x4, waiting for transfers between devices, swap_second(): return lax.ppermute(value, ('rows', 'cols'), second_pairs)  5.18 us
    ppermute x6, starting transfers between devices, swap_first(): return lax.ppermute(value, ('rows', 'cols'), first_pairs)  4.26 us
    pallas_call x1, Pallas kernels, update_matrix(): call(body, pltpu.VMEM((6 * picks, width), BF16), [whole()] * 3, whole(),...  3.7 us
    unnamed x6, local copies, waits for them, and re-layouts  3.39 us
  transfers between devices with their start and end apart: 10, of which 4 were waited for; matrix products, arithmetic and copies ran while one was open for 0% of the time, Pallas kernels for 20%

profile of v2, /device:TPU:0, one launch (start us, length us, event | category | flops | bytes accessed | tf_op | source)
XLA Modules:
  0.0 65.0 jit_solution(4438333847568890309)
XLA Ops:
  0.0 2.3 %own_picks.1 = (f32[32,2,512]{2,1,0:T(2,128)S(1)}, bf16[2,1024,512]{2,1,0:T(8,128)(2,1)S(1)}) custom-call(s32[2,32]{1,0:T(2,128)} %picks_ref.1, bf16[8192,512]{1,0:T(8,128)(2,1)} %refs_0_.7), custom_call_target="tpu_custom_call" | custom-call | bytes 3000000 | tf_op jit(solution)/shard_map/own_picks/pallas_call | solution.py:122
  2.3 15.0 %all_to_all.5 = f32[32,2,512]{2,1,0:T(2,128)S(1)} all-to-all(f32[32,2,512]{2,1,0:T(2,128)S(1)} %get-tuple-element.11), channel_id=1, replica_groups=mesh['rows'=32,'cols'=4] {'rows'}, dimensions={0} | all-to-all | bytes 262144 | tf_op jit(solution)/shard_map/all_to_all | solution.py:371
  17.3 0.1 reshape.3.panel_ref
  17.4 0.7 %given_first.1.mine_ref._ = f32[1056,128]{1,0:T(8,128)S(1)} custom-call(bf16[2,1024,512]{2,1,0:T(8,128)(2,1)S(1)} %get-tuple-element.12.ahead_ref, f32[64,512]{1,0:T(8,128)S(1)} %reshape.3.panel_ref), custom_call_target="tpu_custom_call" | custom-call | bytes 3000000 | tf_op jit(solution)/shard_map/given_first/pallas_call | solution.py:163
  18.1 2.0 %collective-permute-start = (f32[1056,128]{1,0:T(8,128)S(1)}, f32[1056,128]{1,0:T(8,128)S(1)}, u32[]{:S(2)}, u32[]{:S(2)}) collective-permute-start(f32[1056,128]{1,0:T(8,128)S(1)} %given_first.1.mine_ref._), channel_id=1, source_target_pairs={{0,1},{1,0},{2,3},{3,2},{4,7},{5,6},{6,5},{7,4},{8,9},{9,8},{10,11... | collective-permute-start | bytes 1622024 | tf_op jit(solution)/shard_map/ppermute | solution.py:365
  20.1 0.0 copy-start
  20.1 3.4 %copy-done = bf16[8192,512]{1,0:T(8,128)(2,1)S(1)} copy-done((bf16[8192,512]{1,0:T(8,128)(2,1)S(1)}, bf16[8192,512]{1,0:T(8,128)(2,1)}, u32[]{:S(2)}) %copy-start) | copy-done | bytes 8388632
  23.5 0.0 slice-start
  23.5 0.7 %given_rest.1.mine_ref = f32[1024,128]{1,0:T(8,128)S(1)} custom-call(bf16[8192,512]{1,0:T(8,128)(2,1)S(1)} %copy-done, f32[64,512]{1,0:T(8,128)S(1)} %reshape.3.panel_ref, f32[1056,128]{1,0:T(8,128)S(1)} %given_first.1.mine_ref._), custom_call_target="tpu_custom_call" | custom-call | bytes 3000000 | tf_op jit(solution)/shard_map/given_rest/pallas_call | solution.py:186
  24.2 0.0 slice-start.1
  24.2 0.2 collective-permute-start.2
  24.4 3.2 %collective-permute-done.got_ref = f32[1056,128]{1,0:T(8,128)S(1)} collective-permute-done((f32[1056,128]{1,0:T(8,128)S(1)}, f32[1056,128]{1,0:T(8,128)S(1)}, u32[]{:S(2)}, u32[]{:S(2)}) %collective-permute-start) | collective-permute-done | bytes 540704 | tf_op jit(solution)/shard_map/ppermute | solution.py:365
  27.6 0.7 %kept_products.2 = (f32[544,128]{1,0:T(8,128)S(1)}, f32[512,128]{1,0:T(8,128)S(1)}) custom-call(bf16[8192,512]{1,0:T(8,128)(2,1)S(1)} %copy-done, f32[64,512]{1,0:T(8,128)S(1)} %reshape.3.panel_ref, f32[1056,128]{1,0:T(8,128)S(1)} %collective-permute-done.got_ref, f32[1056,128]{1,0:T(8,128)S(1)} %given_first.1.mine_ref._), custom_call_target="tpu_custom_call" | custom-call | bytes 3000000 | tf_op jit(solution)/shard_map/kept_products/pallas_call | solution.py:206
  28.3 4.1 %collective-permute-start.1 = (f32[544,128]{1,0:T(8,128)S(1)}, f32[544,128]{1,0:T(8,128)S(1)}, u32[]{:S(2)}, u32[]{:S(2)}) collective-permute-start(f32[544,128]{1,0:T(8,128)S(1)} %get-tuple-element.13.sent_ref), channel_id=1, source_target_pairs={{0,3},{1,2},{2,1},{3,0},{4,5},{5,4},{6,7},{7,6},{8,11},{9,10},{10,... | collective-permute-start | bytes 835592 | tf_op jit(solution)/shard_map/ppermute | solution.py:368
  32.4 2.8 %collective-permute-done.2.got_ref = f32[1024,128]{1,0:T(8,128)S(1)} collective-permute-done((f32[1024,128]{1,0:T(8,128)S(1)}, f32[1024,128]{1,0:T(8,128)S(1)}, u32[]{:S(2)}, u32[]{:S(2)}) %collective-permute-start.2) | collective-permute-done | bytes 524320 | tf_op jit(solution)/shard_map/ppermute | solution.py:365
  35.2 0.7 %kept_products.3 = (f32[512,128]{1,0:T(8,128)S(1)}, f32[512,128]{1,0:T(8,128)S(1)}) custom-call(bf16[8192,512]{1,0:T(8,128)(2,1)S(1)} %copy-done, f32[64,512]{1,0:T(8,128)S(1)} %reshape.3.panel_ref, f32[1024,128]{1,0:T(8,128)S(1)} %collective-permute-done.2.got_ref, f32[1024,128]{1,0:T(8,128)S(1)} %given_rest.1.mine_ref), custom_call_target="tpu_custom_call" | custom-call | bytes 3000000 | tf_op jit(solution)/shard_map/kept_products/pallas_call | solution.py:206
  35.9 4.1 %collective-permute-start.3 = (f32[512,128]{1,0:T(8,128)S(1)}, f32[512,128]{1,0:T(8,128)S(1)}, u32[]{:S(2)}, u32[]{:S(2)}) collective-permute-start(f32[512,128]{1,0:T(8,128)S(1)} %get-tuple-element.15), channel_id=1, source_target_pairs={{0,3},{1,2},{2,1},{3,0},{4,5},{5,4},{6,7},{7,6},{8,11},{9,10},{10,... | collective-permute-start | bytes 786440 | tf_op jit(solution)/shard_map/ppermute | solution.py:368
  40.0 0.0 collective-permute-done.1.got_ref
  40.1 0.6 collective-permute-start.8
  40.7 3.7 %update_matrix.1.refs_0_.refs_1_ = bf16[384,512]{1,0:T(8,128)(2,1)S(1)} custom-call(f32[544,128]{1,0:T(8,128)S(1)} %get-tuple-element.13.sent_ref, f32[544,128]{1,0:T(8,128)S(1)} %collective-permute-done.1.got_ref, f32[64,512]{1,0:T(8,128)S(1)} %reshape.3.panel_ref), custom_call_target="tpu_custom_call" | custom-call | bytes 3000000 | tf_op jit(solution)/shard_map/update_matrix/pallas_call | solution.py:288
  44.4 0.0 collective-permute-done.3.got_ref
  44.4 3.3 %collective-permute-start.5 = (f32[512,128]{1,0:T(8,128)S(1)}, f32[512,128]{1,0:T(8,128)S(1)}, u32[]{:S(2)}, u32[]{:S(2)}) collective-permute-start(f32[512,128]{1,0:T(8,128)S(1)} %added.2.refs_2_), channel_id=1, source_target_pairs={{0,3},{1,2},{2,1},{3,0},{4,5},{5,4},{6,7},{7,6},{8,11},{9,10},{10,... | collective-permute-start | bytes 786440 | tf_op jit(solution)/shard_map/ppermute | solution.py:368
  47.7 0.0 collective-permute-start.7
  47.7 0.0 collective-permute-done.8.refs_3_
  47.7 2.0 %collective-permute-start.9 = (f32[512,128]{1,0:T(8,128)S(1)}, f32[512,128]{1,0:T(8,128)S(1)}, u32[]{:S(2)}, u32[]{:S(2)}) collective-permute-start(f32[512,128]{1,0:T(8,128)S(1)} %collective-permute-done.8.refs_3_), channel_id=1, source_target_pairs={{0,1},{1,0},{2,3},{3,2},{4,7},{5,6},{6,5},{7,4},{8,9},{9,8},{10,11... | collective-permute-start | bytes 786440 | tf_op jit(solution)/shard_map/ppermute | solution.py:365
  49.8 0.0 collective-permute-start.4
  49.8 5.2 %collective-permute-done.5.refs_3_ = f32[512,128]{1,0:T(8,128)S(1)} collective-permute-done((f32[512,128]{1,0:T(8,128)S(1)}, f32[512,128]{1,0:T(8,128)S(1)}, u32[]{:S(2)}, u32[]{:S(2)}) %collective-permute-start.5) | collective-permute-done | bytes 262176 | tf_op jit(solution)/shard_map/ppermute | solution.py:368
  55.0 0.0 collective-permute-start.6
  55.0 0.0 slice-done
  55.0 0.0 slice-done.1
  55.0 2.4 %update_near.2.refs_4_ = f32[8192,512]{1,0:T(8,128)} custom-call(bf16[8192,512]{1,0:T(8,128)(2,1)S(1)} %bitcast.1, bf16[384,512]{1,0:T(8,128)(2,1)S(1)} %update_matrix.1.refs_0_.refs_1_, f32[512,128]{1,0:T(8,128)S(1)} %added.3.refs_2_, f32[512,128]{1,0:T(8,128)S(1)} %collective-permute-done.8.refs_3_), custom_call_target="tpu_custom_call" | custom-call | bytes 3000000 | tf_op jit(solution)/shard_map/update_near/pallas_call | solution.py:345
  57.4 2.4 %update_near.3.refs_4_ = f32[8192,512]{1,0:T(8,128)} custom-call(bf16[8192,512]{1,0:T(8,128)(2,1)S(1)} %bitcast.1, bf16[384,512]{1,0:T(8,128)(2,1)S(1)} %update_matrix.1.refs_0_.refs_1_, f32[512,128]{1,0:T(8,128)S(1)} %added.2.refs_2_, f32[512,128]{1,0:T(8,128)S(1)} %collective-permute-done.5.refs_3_, ...), custom_call_target="tpu_custom_call", output_to_operand_aliasing={{}: (4, {})} | custom-call | bytes 3000000 | tf_op jit(solution)/shard_map/update_near/pallas_call | solution.py:345
  59.9 0.0 collective-permute-done.7.refs_2_
  59.9 0.0 collective-permute-done.9.refs_3_
  59.9 2.4 %update_far.2.refs_4_ = f32[8192,512]{1,0:T(8,128)} custom-call(bf16[8192,512]{1,0:T(8,128)(2,1)S(1)} %bitcast.1, bf16[384,512]{1,0:T(8,128)(2,1)S(1)} %update_matrix.1.refs_0_.refs_1_, f32[512,128]{1,0:T(8,128)S(1)} %collective-permute-done.7.refs_2_, f32[512,128]{1,0:T(8,128)S(1)} %collective-permute-done.9.refs_3_, ...), custom_call_target="tpu_custom_call", output_to_operand_aliasing={{}: (4, {})} | custom-call | bytes 3000000 | tf_op jit(solution)/shard_map/update_far/pallas_call | solution.py:345
  62.3 0.0 collective-permute-done.4.refs_2_
  62.3 0.2 collective-permute-done.6.refs_3_
  62.5 2.4 %update_far.3 = f32[8192,512]{1,0:T(8,128)} custom-call(bf16[8192,512]{1,0:T(8,128)(2,1)S(1)} %bitcast.1, bf16[384,512]{1,0:T(8,128)(2,1)S(1)} %update_matrix.1.refs_0_.refs_1_, f32[512,128]{1,0:T(8,128)S(1)} %collective-permute-done.4.refs_2_, f32[512,128]{1,0:T(8,128)S(1)} %collective-permute-done.6.refs_3_, ...), custom_call_target="tpu_custom_call", output_to_operand_aliasing={{}: (4, {})} | custom-call | bytes 3000000 | tf_op jit(solution)/shard_map/update_far/pallas_call | solution.py:345
  (3 shorter events, 0.1 us)
Async XLA Ops:
  18.1 9.4 %collective-permute-start = (f32[1056,128]{1,0:T(8,128)S(1)}, f32[1056,128]{1,0:T(8,128)S(1)}, u32[]{:S(2)}, u32[]{:S(2)}) collective-permute-start(f32[1056,128]{1,0:T(8,128)S(1)} %given_first.1.mine_ref._), channel_id=1, source_target_pairs={{0,1},{1,0},{2,3},{3,2},{4,7},{5,6},{6,5},{7,4},{8,9},{9,8},{10,11... | collective-permute-start | bytes 1622024 | tf_op jit(solution)/shard_map/ppermute | solution.py:365
  20.1 3.4 %copy-start = (bf16[8192,512]{1,0:T(8,128)(2,1)S(1)}, bf16[8192,512]{1,0:T(8,128)(2,1)}, u32[]{:S(2)}) copy-start(bf16[8192,512]{1,0:T(8,128)(2,1)} %refs_0_.7) | copy-start | bytes 25165828
  23.5 31.5 %slice-start = ((s8[8388608]{0:T(1024)(128)(4,1)}), s8[4194304]{0:T(1024)(128)(4,1)S(1)}, s32[]{:S(2)}) async-start(s8[8388608]{0:T(1024)(128)(4,1)} %bitcast), calls=%async_computation.1 | async-start | bytes 8388608
  24.2 30.8 %slice-start.1 = ((s8[8388608]{0:T(1024)(128)(4,1)}), s8[4194304]{0:T(1024)(128)(4,1)S(1)}, s32[]{:S(2)}) async-start(s8[8388608]{0:T(1024)(128)(4,1)} %bitcast), calls=%async_computation.2 | async-start | bytes 8388608
  24.2 11.0 %collective-permute-start.2 = (f32[1024,128]{1,0:T(8,128)S(1)}, f32[1024,128]{1,0:T(8,128)S(1)}, u32[]{:S(2)}, u32[]{:S(2)}) collective-permute-start(f32[1024,128]{1,0:T(8,128)S(1)} %given_rest.1.mine_ref), channel_id=1, source_target_pairs={{0,1},{1,0},{2,3},{3,2},{4,7},{5,6},{6,5},{7,4},{8,9},{9,8},{10,11... | collective-permute-start | bytes 1572872 | tf_op jit(solution)/shard_map/ppermute | solution.py:365
  28.3 11.8 %collective-permute-start.1 = (f32[544,128]{1,0:T(8,128)S(1)}, f32[544,128]{1,0:T(8,128)S(1)}, u32[]{:S(2)}, u32[]{:S(2)}) collective-permute-start(f32[544,128]{1,0:T(8,128)S(1)} %get-tuple-element.13.sent_ref), channel_id=1, source_target_pairs={{0,3},{1,2},{2,1},{3,0},{4,5},{5,4},{6,7},{7,6},{8,11},{9,10},{10,... | collective-permute-start | bytes 835592 | tf_op jit(solution)/shard_map/ppermute | solution.py:368
  35.9 8.5 %collective-permute-start.3 = (f32[512,128]{1,0:T(8,128)S(1)}, f32[512,128]{1,0:T(8,128)S(1)}, u32[]{:S(2)}, u32[]{:S(2)}) collective-permute-start(f32[512,128]{1,0:T(8,128)S(1)} %get-tuple-element.15), channel_id=1, source_target_pairs={{0,3},{1,2},{2,1},{3,0},{4,5},{5,4},{6,7},{7,6},{8,11},{9,10},{10,... | collective-permute-start | bytes 786440 | tf_op jit(solution)/shard_map/ppermute | solution.py:368
  40.1 7.7 %collective-permute-start.8 = (f32[512,128]{1,0:T(8,128)S(1)}, f32[512,128]{1,0:T(8,128)S(1)}, u32[]{:S(2)}, u32[]{:S(2)}) collective-permute-start(f32[512,128]{1,0:T(8,128)S(1)} %added.3.refs_2_), channel_id=1, source_target_pairs={{0,3},{1,2},{2,1},{3,0},{4,5},{5,4},{6,7},{7,6},{8,11},{9,10},{10,... | collective-permute-start | bytes 786440 | tf_op jit(solution)/shard_map/ppermute | solution.py:368
  44.4 10.5 %collective-permute-start.5 = (f32[512,128]{1,0:T(8,128)S(1)}, f32[512,128]{1,0:T(8,128)S(1)}, u32[]{:S(2)}, u32[]{:S(2)}) collective-permute-start(f32[512,128]{1,0:T(8,128)S(1)} %added.2.refs_2_), channel_id=1, source_target_pairs={{0,3},{1,2},{2,1},{3,0},{4,5},{5,4},{6,7},{7,6},{8,11},{9,10},{10,... | collective-permute-start | bytes 786440 | tf_op jit(solution)/shard_map/ppermute | solution.py:368
  47.7 12.1 %collective-permute-start.7 = (f32[512,128]{1,0:T(8,128)S(1)}, f32[512,128]{1,0:T(8,128)S(1)}, u32[]{:S(2)}, u32[]{:S(2)}) collective-permute-start(f32[512,128]{1,0:T(8,128)S(1)} %added.3.refs_2_), channel_id=1, source_target_pairs={{0,1},{1,0},{2,3},{3,2},{4,7},{5,6},{6,5},{7,4},{8,9},{9,8},{10,11... | collective-permute-start | bytes 786440 | tf_op jit(solution)/shard_map/ppermute | solution.py:365
  47.7 12.1 %collective-permute-start.9 = (f32[512,128]{1,0:T(8,128)S(1)}, f32[512,128]{1,0:T(8,128)S(1)}, u32[]{:S(2)}, u32[]{:S(2)}) collective-permute-start(f32[512,128]{1,0:T(8,128)S(1)} %collective-permute-done.8.refs_3_), channel_id=1, source_target_pairs={{0,1},{1,0},{2,3},{3,2},{4,7},{5,6},{6,5},{7,4},{8,9},{9,8},{10,11... | collective-permute-start | bytes 786440 | tf_op jit(solution)/shard_map/ppermute | solution.py:365
  49.8 12.6 %collective-permute-start.4 = (f32[512,128]{1,0:T(8,128)S(1)}, f32[512,128]{1,0:T(8,128)S(1)}, u32[]{:S(2)}, u32[]{:S(2)}) collective-permute-start(f32[512,128]{1,0:T(8,128)S(1)} %added.2.refs_2_), channel_id=1, source_target_pairs={{0,1},{1,0},{2,3},{3,2},{4,7},{5,6},{6,5},{7,4},{8,9},{9,8},{10,11... | collective-permute-start | bytes 786440 | tf_op jit(solution)/shard_map/ppermute | solution.py:365
  55.0 7.6 %collective-permute-start.6 = (f32[512,128]{1,0:T(8,128)S(1)}, f32[512,128]{1,0:T(8,128)S(1)}, u32[]{:S(2)}, u32[]{:S(2)}) collective-permute-start(f32[512,128]{1,0:T(8,128)S(1)} %collective-permute-done.5.refs_3_), channel_id=1, source_target_pairs={{0,1},{1,0},{2,3},{3,2},{4,7},{5,6},{6,5},{7,4},{8,9},{9,8},{10,11... | collective-permute-start | bytes 786440 | tf_op jit(solution)/shard_map/ppermute | solution.py:365

commit v3 on v2

--- a/solution.py
+++ b/solution.py
@@ -95,6 +95,8 @@
                         ahead_sems.at[2 * j + g],
                     )
                 )
+        for move in moves:
+            move.start()
         load.wait()
         first = lax.axis_index("rows") * rows
         offsets, found = [], []
@@ -108,8 +110,6 @@
             move = pltpu.make_async_copy(emb_ref.at[pl.ds(base, tile), :], held.at[r], sems.at[r])
             move.start()
             found.append(move)
-        for move in moves:
-            move.start()
         for r in range(rounds):
             found[r].wait()
             block = held[r].astype(F32)
@@ -170,22 +170,23 @@
     return paired_products(emb_ref[pl.ds(start, size), :], emb_ref[pl.ds(start + size, size), :], paired)
 
 
-def given_rest(emb, panel, block_rows, chunks, after):
+def given_rest(emb, panel, block_rows, k, after):
     picks = panel.shape[0]
-
-    def body(emb_ref, panel_ref, _, *out_refs):
+    size = CHUNKS[k]
+
+    def body(emb_ref, panel_ref, _, pass_ref, own_ref):
         half, _, quarter = kept()
         paired = paired_panel(panel_ref[...])
-        for out_ref, k in zip(out_refs, chunks):
-            size = CHUNKS[k]
-            for j in range(2):
-                start = block_start(1 - half, quarter if j else 1 - quarter, block_rows, k)
-                out_ref[j * size : (j + 1) * size, :] = quarter_products(emb_ref, start, size, paired)
-
-    shapes = [pltpu.VMEM((2 * CHUNKS[k], 2 * picks), F32) for k in chunks]
-    return call(body, shapes, [whole(), whole(), anywhere()], [whole()] * len(shapes), name="given_rest")(
-        emb, in_vmem(panel), after
-    )
+        pass_ref[...] = quarter_products(emb_ref, block_start(1 - half, 1 - quarter, block_rows, k), size, paired)
+        own_ref[...] = quarter_products(emb_ref, block_start(1 - half, quarter, block_rows, k), size, paired)
+
+    return call(
+        body,
+        [pltpu.VMEM((size, 2 * picks), F32)] * 2,
+        [whole(), whole(), anywhere()],
+        [whole()] * 2,
+        name="given_rest",
+    )(emb, in_vmem(panel), after)
 
 
 def kept_products(emb, panel, got, message, block_rows, k):
@@ -200,8 +201,8 @@
         out_ref[:size, :] = quarter_products(emb_ref, start, size, paired) + got_ref[:size, :]
         if extra:
             out_ref[size:, :] = got_ref[2 * size :, :] + mine_ref[2 * size :, :]
-        start = block_start(half, quarter, block_rows, k)
-        own_ref[...] = quarter_products(emb_ref, start, size, paired) + got_ref[size : 2 * size, :]
+        own = quarter_products(emb_ref, block_start(half, quarter, block_rows, k), size, paired)
+        own_ref[...] = own + got_ref[size : 2 * size, :] if extra else own
 
     return call(
         body,
@@ -212,27 +213,33 @@
     )(emb, in_vmem(panel), in_vmem(got), in_vmem(message))
 
 
-def added(own, got, after):
-    def body(own_ref, got_ref, *refs):
-        refs[-1][...] = own_ref[...] + got_ref[: own.shape[0], :]
-
-    return call(
-        body, pltpu.VMEM(own.shape, F32), [whole(), whole()] + [anywhere()] * len(after), whole(), name="added"
-    )(in_vmem(own), in_vmem(got), *after)
-
-
-def stacked(top, bottom, after):
-    def body(top_ref, bottom_ref, *refs):
-        refs[-1][: top.shape[0], :] = top_ref[...]
-        refs[-1][top.shape[0] :, :] = bottom_ref[...]
-
-    return call(
-        body,
-        pltpu.VMEM((top.shape[0] + bottom.shape[0], top.shape[1]), F32),
-        [whole(), whole()] + [anywhere()] * len(after),
+def added(parts, after):
+    shape = parts[0].shape
+
+    def body(*refs):
+        total = refs[0][...]
+        for ref in refs[1 : len(parts)]:
+            total = total + ref[: shape[0], :]
+        refs[-1][...] = total
+
+    count = len(parts) + len(after)
+    return call(body, pltpu.VMEM(shape, F32), [whole()] * count, whole(), name="added")(
+        *[in_vmem(p) for p in parts], *[in_vmem(a) for a in after]
+    )
+
+
+def in_order(value, *after):
+    def body(*refs):
+        pass
+
+    return call(
+        body,
+        pltpu.VMEM(value.shape, F32),
+        [whole()] * (1 + len(after)),
         whole(),
-        name="stacked",
-    )(in_vmem(top), in_vmem(bottom), *after)
+        aliases={len(after): 0},
+        name="in_order",
+    )(*[in_vmem(a) for a in after], in_vmem(value))
 
 
 def split(value):
@@ -290,7 +297,7 @@
     )
 
 
-def update(emb, right, out, pieces, block_rows, name):
+def update(emb, right, out, pieces, block_rows, name, token=False):
     rows, width = emb.shape
     picks = right.shape[0] // 6
     steps = []
@@ -303,7 +310,10 @@
 
     def body(*refs):
         emb_ref, right_ref = refs[:2]
-        out_ref, staged, sems = refs[-3:]
+        staged, sems = refs[-2:]
+        out_ref = refs[-4 if token else -3]
+        if token:
+            refs[-3][...] = jnp.zeros_like(refs[-3])
         half, quarter, partner_quarter = kept()
         right_mat = right_ref[...]
         moves = []
@@ -344,9 +354,9 @@
         aliases = {len(operands) - 1: 0}
     return call(
         body,
-        jax.ShapeDtypeStruct((rows, width), F32),
+        [jax.ShapeDtypeStruct((rows, width), F32)] + [pltpu.VMEM((8, 128), F32)] * token,
         specs,
-        anywhere(),
+        [anywhere()] + [whole()] * token,
         [pltpu.VMEM((len(steps), biggest, width), F32), pltpu.SemaphoreType.DMA((len(steps),))],
         aliases,
         name=name,
@@ -370,25 +380,34 @@
     mine, ahead = own_picks(emb, pick_rows, owners, block_rows)
     panel = lax.all_to_all(mine, "rows", 0, 0, tiled=True).reshape(owners * rounds, width)
 
-    messages = [given_first(ahead, panel)]
-    messages += given_rest(emb, panel, block_rows, list(range(1, count)), messages[0])
-    halves = [swap_first(m) for m in messages]
-    sent, own = zip(*[kept_products(emb, panel, halves[k], messages[k], block_rows, k) for k in range(count)])
+    message = given_first(ahead, panel)
+    got = swap_first(message)
+    passing, staying = given_rest(emb, panel, block_rows, 1, message)
+    next_got, staying = swap_first(passing), swap_first(staying)
+    sent, own = zip(
+        kept_products(emb, panel, got, message, block_rows, 0), kept_products(emb, panel, next_got, passing, block_rows, 1)
+    )
     quarters = [swap_second(m) for m in sent]
     right = update_matrix(sent[0], quarters[0], panel)
 
-    totals, near, far = [], [], []
-    for k in range(count):
-        totals.append(added(own[k], quarters[k], [right] if k else []))
-        near.append(swap_second(totals[k]))
-    for k in range(count):
-        far.append((swap_first(totals[k]), swap_first(near[k])))
-    out = None
-    for k in range(count):
-        out = update(emb, right, out, [(totals[k], 0, k, False, True), (near[k], 0, k, False, False)], block_rows, "update_near")
-    for k in range(count):
-        pieces = [(far[k][0], 0, k, True, True), (far[k][1], 0, k, True, False)]
-        out = update(emb, right, out, pieces, block_rows, "update_far")
+    totals = [added([own[0], quarters[0]], [staying]), added([own[1], staying, quarters[1]], [right])]
+    near = [swap_second(t) for t in totals]
+    theirs = [swap_first(t) for t in totals]
+    last = count - 1
+    across = []
+    for k in range(last):
+        near[k] = in_order(near[k], theirs[k])
+        across.append(swap_first(near[k]))
+    pieces = [(totals[k], 0, k, False, True) for k in range(count)]
+    pieces += [(near[k], 0, k, False, False) for k in range(last)]
+    out, token = update(emb, right, None, pieces, block_rows, "update_near", True)
+    near[last] = in_order(near[last], token)
+    across.append(swap_first(near[last]))
+    pieces = [(near[last], 0, last, False, False)]
+    pieces += [(theirs[k], 0, k, True, True) for k in range(count)]
+    pieces += [(across[k], 0, k, True, False) for k in range(last)]
+    (out,) = update(emb, right, out, pieces, block_rows, "update_far")
+    (out,) = update(emb, right, out, [(across[last], 0, last, True, False)], block_rows, "update_last")
     return out
 
 

time: 65.7 us -> 64.4 us (0.980)
  waiting for transfers between devices: 11.3 us -> 14 us
  Pallas kernels: 18.6 us -> 16.9 us
  starting transfers between devices: 16.4 us -> 14.7 us
    ppermute x6 -> x7, waiting for transfers between devices: 6.17 us -> 11.2 us  [swap_first(): return lax.ppermute(value, ('rows', 'cols'), first_pairs)]
    ppermute x4, starting transfers between devices: 12.2 us -> 9.62 us  [swap_second(): return lax.ppermute(value, ('rows', 'cols'), second_pairs)]
    ppermute x4, waiting for transfers between devices: 5.18 us -> 2.79 us  [swap_second(): return lax.ppermute(value, ('rows', 'cols'), second_pairs)]
    pallas_call x7 -> x8, Pallas kernels: 10.4 us -> 9.35 us  [the longest x3 8.59 us: update(): call(body, [jax.ShapeDtypeStruct((rows, width), F32)] + [pltpu.VMEM((8, 1...]
    ppermute x6 -> x7, starting transfers between devices: 4.26 us -> 5.08 us  [swap_first(): return lax.ppermute(value, ('rows', 'cols'), first_pairs)]
  transfers between devices with their start and end apart: 10 -> 11, of which waited for: 4 -> 5; matrix products, arithmetic and copies ran while one was open for 0% -> 0% of each run, Pallas kernels for 20% -> 20%
where the time goes in v3:
time: 64.4 us; the launch traced here: 64.2 us
  Pallas kernels  16.9 us (26%)
  blocking collectives  15 us (23%)
  starting transfers between devices  14.7 us (23%)
  waiting for transfers between devices  14 us (22%)
  local copies, waits for them, and re-layouts  3.48 us (5%)
    all_to_all x1, blocking collectives, per_device(): lax.all_to_all(mine, 'rows', 0, 0, tiled=True)  15 us
    ppermute x7, waiting for transfers between devices, swap_first(): return lax.ppermute(value, ('rows', 'cols'), first_pairs)  11.2 us
    ppermute x4, starting transfers between devices, swap_second(): return lax.ppermute(value, ('rows', 'cols'), second_pairs)  9.62 us
    pallas_call x3, Pallas kernels, update(): call(body, [jax.ShapeDtypeStruct((rows, width), F32)] + [pltpu.VMEM((8, 1...  8.59 us
    ppermute x7, starting transfers between devices, swap_first(): return lax.ppermute(value, ('rows', 'cols'), first_pairs)  5.08 us
    pallas_call x1, Pallas kernels, update_matrix(): call(body, pltpu.VMEM((6 * picks, width), BF16), [whole()] * 3, whole(),...  3.71 us
    unnamed x6, local copies, waits for them, and re-layouts  3.39 us
    ppermute x4, waiting for transfers between devices, swap_second(): return lax.ppermute(value, ('rows', 'cols'), second_pairs)  2.79 us
  transfers between devices with their start and end apart: 11, of which 5 were waited for; matrix products, arithmetic and copies ran while one was open for 0% of the time, Pallas kernels for 20%

profile of v3, /device:TPU:0, one launch (start us, length us, event | category | flops | bytes accessed | tf_op | source)
XLA Modules:
  0.0 64.2 jit_solution(14012695344311518011)
XLA Ops:
  0.0 1.8 %own_picks.1 = (f32[32,2,512]{2,1,0:T(2,128)S(1)}, bf16[2,1024,512]{2,1,0:T(8,128)(2,1)S(1)}) custom-call(s32[2,32]{1,0:T(2,128)} %picks_ref.1, bf16[8192,512]{1,0:T(8,128)(2,1)} %refs_0_.5), custom_call_target="tpu_custom_call" | custom-call | bytes 3000000 | tf_op jit(solution)/shard_map/own_picks/pallas_call | solution.py:122
  1.8 15.0 %all_to_all.5 = f32[32,2,512]{2,1,0:T(2,128)S(1)} all-to-all(f32[32,2,512]{2,1,0:T(2,128)S(1)} %get-tuple-element.15), channel_id=1, replica_groups=mesh['rows'=32,'cols'=4] {'rows'}, dimensions={0} | all-to-all | bytes 262144 | tf_op jit(solution)/shard_map/all_to_all | solution.py:381
  16.8 0.1 reshape.3.panel_ref
  16.9 0.7 %given_first.1.mine_ref._ = f32[1056,128]{1,0:T(8,128)S(1)} custom-call(bf16[2,1024,512]{2,1,0:T(8,128)(2,1)S(1)} %get-tuple-element.16.ahead_ref, f32[64,512]{1,0:T(8,128)S(1)} %reshape.3.panel_ref), custom_call_target="tpu_custom_call" | custom-call | bytes 3000000 | tf_op jit(solution)/shard_map/given_first/pallas_call | solution.py:163
  17.6 2.0 %collective-permute-start = (f32[1056,128]{1,0:T(8,128)S(1)}, f32[1056,128]{1,0:T(8,128)S(1)}, u32[]{:S(2)}, u32[]{:S(2)}) collective-permute-start(f32[1056,128]{1,0:T(8,128)S(1)} %given_first.1.mine_ref._), channel_id=1, source_target_pairs={{0,1},{1,0},{2,3},{3,2},{4,7},{5,6},{6,5},{7,4},{8,9},{9,8},{10,11... | collective-permute-start | bytes 1622024 | tf_op jit(solution)/shard_map/ppermute | solution.py:375
  19.6 0.0 copy-start
  19.6 3.4 %copy-done = bf16[8192,512]{1,0:T(8,128)(2,1)S(1)} copy-done((bf16[8192,512]{1,0:T(8,128)(2,1)S(1)}, bf16[8192,512]{1,0:T(8,128)(2,1)}, u32[]{:S(2)}) %copy-start) | copy-done | bytes 8388632
  23.0 0.0 slice-start
  23.0 0.7 %given_rest.1 = (f32[512,128]{1,0:T(8,128)S(1)}, f32[512,128]{1,0:T(8,128)S(1)}) custom-call(bf16[8192,512]{1,0:T(8,128)(2,1)S(1)} %copy-done, f32[64,512]{1,0:T(8,128)S(1)} %reshape.3.panel_ref, f32[1056,128]{1,0:T(8,128)S(1)} %given_first.1.mine_ref._), custom_call_target="tpu_custom_call" | custom-call | bytes 3000000 | tf_op jit(solution)/shard_map/given_rest/pallas_call | solution.py:183
  23.7 0.0 slice-start.1
  23.7 0.2 collective-permute-start.3
  23.9 3.2 %collective-permute-done.got_ref = f32[1056,128]{1,0:T(8,128)S(1)} collective-permute-done((f32[1056,128]{1,0:T(8,128)S(1)}, f32[1056,128]{1,0:T(8,128)S(1)}, u32[]{:S(2)}, u32[]{:S(2)}) %collective-permute-start) | collective-permute-done | bytes 540704 | tf_op jit(solution)/shard_map/ppermute | solution.py:375
  27.1 0.7 %kept_products.2 = (f32[544,128]{1,0:T(8,128)S(1)}, f32[512,128]{1,0:T(8,128)S(1)}) custom-call(bf16[8192,512]{1,0:T(8,128)(2,1)S(1)} %copy-done, f32[64,512]{1,0:T(8,128)S(1)} %reshape.3.panel_ref, f32[1056,128]{1,0:T(8,128)S(1)} %collective-permute-done.got_ref, f32[1056,128]{1,0:T(8,128)S(1)} %given_first.1.mine_ref._), custom_call_target="tpu_custom_call" | custom-call | bytes 3000000 | tf_op jit(solution)/shard_map/kept_products/pallas_call | solution.py:207
  27.8 4.1 %collective-permute-start.1 = (f32[544,128]{1,0:T(8,128)S(1)}, f32[544,128]{1,0:T(8,128)S(1)}, u32[]{:S(2)}, u32[]{:S(2)}) collective-permute-start(f32[544,128]{1,0:T(8,128)S(1)} %get-tuple-element.17.sent_ref), channel_id=1, source_target_pairs={{0,3},{1,2},{2,1},{3,0},{4,5},{5,4},{6,7},{7,6},{8,11},{9,10},{10,... | collective-permute-start | bytes 835592 | tf_op jit(solution)/shard_map/ppermute | solution.py:378
  31.9 0.0 collective-permute-start.2
  31.9 0.0 collective-permute-done.3.got_ref
  31.9 0.7 %kept_products.3 = (f32[512,128]{1,0:T(8,128)S(1)}, f32[512,128]{1,0:T(8,128)S(1)}) custom-call(bf16[8192,512]{1,0:T(8,128)(2,1)S(1)} %copy-done, f32[64,512]{1,0:T(8,128)S(1)} %reshape.3.panel_ref, f32[512,128]{1,0:T(8,128)S(1)} %collective-permute-done.3.got_ref, f32[512,128]{1,0:T(8,128)S(1)} %get-tuple-element.20.mine_ref), custom_call_target="tpu_custom_call" | custom-call | bytes 3000000 | tf_op jit(solution)/shard_map/kept_products/pallas_call | solution.py:207
  32.6 2.1 %collective-permute-start.4 = (f32[512,128]{1,0:T(8,128)S(1)}, f32[512,128]{1,0:T(8,128)S(1)}, u32[]{:S(2)}, u32[]{:S(2)}) collective-permute-start(f32[512,128]{1,0:T(8,128)S(1)} %get-tuple-element.22), channel_id=1, source_target_pairs={{0,3},{1,2},{2,1},{3,0},{4,5},{5,4},{6,7},{7,6},{8,11},{9,10},{10,... | collective-permute-start | bytes 786440 | tf_op jit(solution)/shard_map/ppermute | solution.py:378
  34.7 6.3 %collective-permute-done.2.refs_2_.refs_1_ = f32[512,128]{1,0:T(8,128)S(1)} collective-permute-done((f32[512,128]{1,0:T(8,128)S(1)}, f32[512,128]{1,0:T(8,128)S(1)}, u32[]{:S(2)}, u32[]{:S(2)}) %collective-permute-start.2) | collective-permute-done | bytes 262176 | tf_op jit(solution)/shard_map/ppermute | solution.py:375
  41.0 0.0 collective-permute-done.1.got_ref.refs_1_
  41.0 0.8 %collective-permute-start.6 = (f32[512,128]{1,0:T(8,128)S(1)}, f32[512,128]{1,0:T(8,128)S(1)}, u32[]{:S(2)}, u32[]{:S(2)}) collective-permute-start(f32[512,128]{1,0:T(8,128)S(1)} %added.2.refs_2_), channel_id=1, source_target_pairs={{0,3},{1,2},{2,1},{3,0},{4,5},{5,4},{6,7},{7,6},{8,11},{9,10},{10,... | collective-permute-start | bytes 786440 | tf_op jit(solution)/shard_map/ppermute | solution.py:378
  41.8 0.0 collective-permute-start.5
  41.8 3.7 %update_matrix.1.refs_3_.refs_1_ = bf16[384,512]{1,0:T(8,128)(2,1)S(1)} custom-call(f32[544,128]{1,0:T(8,128)S(1)} %get-tuple-element.17.sent_ref, f32[544,128]{1,0:T(8,128)S(1)} %collective-permute-done.1.got_ref.refs_1_, f32[64,512]{1,0:T(8,128)S(1)} %reshape.3.panel_ref), custom_call_target="tpu_custom_call" | custom-call | bytes 3000000 | tf_op jit(solution)/shard_map/update_matrix/pallas_call | solution.py:295
  45.6 0.0 collective-permute-done.4.refs_2_
  45.6 2.5 %collective-permute-start.7 = (f32[512,128]{1,0:T(8,128)S(1)}, f32[512,128]{1,0:T(8,128)S(1)}, u32[]{:S(2)}, u32[]{:S(2)}) collective-permute-start(f32[512,128]{1,0:T(8,128)S(1)} %added.3.refs_3_), channel_id=1, source_target_pairs={{0,3},{1,2},{2,1},{3,0},{4,5},{5,4},{6,7},{7,6},{8,11},{9,10},{10,... | collective-permute-start | bytes 786440 | tf_op jit(solution)/shard_map/ppermute | solution.py:378
  48.2 1.4 %collective-permute-start.9 = (f32[512,128]{1,0:T(8,128)S(1)}, f32[512,128]{1,0:T(8,128)S(1)}, u32[]{:S(2)}, u32[]{:S(2)}) collective-permute-start(f32[512,128]{1,0:T(8,128)S(1)} %added.3.refs_3_), channel_id=1, source_target_pairs={{0,1},{1,0},{2,3},{3,2},{4,7},{5,6},{6,5},{7,4},{8,9},{9,8},{10,11... | collective-permute-start | bytes 786440 | tf_op jit(solution)/shard_map/ppermute | solution.py:375
  49.6 0.0 collective-permute-done.6.refs_1_
  49.6 0.0 collective-permute-done.5.refs_0_.refs_3_
  49.6 0.6 collective-permute-start.10
  50.2 0.0 slice-done
  50.2 0.0 slice-done.1
  50.2 3.1 %update_near.1 = (f32[8192,512]{1,0:T(8,128)}, f32[8,128]{1,0:T(8,128)S(1)}) custom-call(bf16[8192,512]{1,0:T(8,128)(2,1)S(1)} %bitcast.1, bf16[384,512]{1,0:T(8,128)(2,1)S(1)} %update_matrix.1.refs_3_.refs_1_, f32[512,128]{1,0:T(8,128)S(1)} %added.2.refs_2_, f32[512,128]{1,0:T(8,128)S(1)} %added.3.refs_3_, f32[512,128]{1,0:T(8,128)S(1)} %in_order.2.refs_4_), custom_call_target="tpu_custom_call" | custom-call | bytes 3000000 | tf_op jit(solution)/shard_map/update_near/pallas_call | solution.py:355
  53.3 2.8 %collective-permute-done.7.refs_1_ = f32[512,128]{1,0:T(8,128)S(1)} collective-permute-done((f32[512,128]{1,0:T(8,128)S(1)}, f32[512,128]{1,0:T(8,128)S(1)}, u32[]{:S(2)}, u32[]{:S(2)}) %collective-permute-start.7) | collective-permute-done | bytes 262176 | tf_op jit(solution)/shard_map/ppermute | solution.py:378
  56.1 0.9 %collective-permute-start.8 = (f32[512,128]{1,0:T(8,128)S(1)}, f32[512,128]{1,0:T(8,128)S(1)}, u32[]{:S(2)}, u32[]{:S(2)}) collective-permute-start(f32[512,128]{1,0:T(8,128)S(1)} %in_order.3.refs_2_), channel_id=1, source_target_pairs={{0,1},{1,0},{2,3},{3,2},{4,7},{5,6},{6,5},{7,4},{8,9},{9,8},{10,11... | collective-permute-start | bytes 786440 | tf_op jit(solution)/shard_map/ppermute | solution.py:375
  57.0 0.0 collective-permute-done.9.refs_4_
  57.0 0.4 collective-permute-done.10.refs_5_
  57.3 3.8 %update_far.1.refs_3_ = f32[8192,512]{1,0:T(8,128)} custom-call(bf16[8192,512]{1,0:T(8,128)(2,1)S(1)} %bitcast.1, bf16[384,512]{1,0:T(8,128)(2,1)S(1)} %update_matrix.1.refs_3_.refs_1_, f32[512,128]{1,0:T(8,128)S(1)} %in_order.3.refs_2_, f32[512,128]{1,0:T(8,128)S(1)} %collective-permute-done.5.refs_0_.refs_3_, ...), custom_call_target="tpu_custom_call", output_to_operand_aliasing={{}: (6, {})} | custom-call | bytes 3000000 | tf_op jit(solution)/shard_map/update_far/pallas_call | solution.py:355
  61.1 1.3 %collective-permute-done.8.refs_2_ = f32[512,128]{1,0:T(8,128)S(1)} collective-permute-done((f32[512,128]{1,0:T(8,128)S(1)}, f32[512,128]{1,0:T(8,128)S(1)}, u32[]{:S(2)}, u32[]{:S(2)}) %collective-permute-start.8) | collective-permute-done | bytes 262176 | tf_op jit(solution)/shard_map/ppermute | solution.py:375
  62.5 1.7 %update_last.1 = f32[8192,512]{1,0:T(8,128)} custom-call(bf16[8192,512]{1,0:T(8,128)(2,1)S(1)} %bitcast.1, bf16[384,512]{1,0:T(8,128)(2,1)S(1)} %update_matrix.1.refs_3_.refs_1_, f32[512,128]{1,0:T(8,128)S(1)} %collective-permute-done.8.refs_2_, f32[8192,512]{1,0:T(8,128)} %update_far.1.refs_3_), custom_call_target="tpu_custom_call", output_to_operand_aliasing={{}: (3, {})} | custom-call | bytes 3000000 | tf_op jit(solution)/shard_map/update_last/pallas_call | solution.py:355
  (5 shorter events, 0.1 us)
Async XLA Ops:
  17.6 9.4 %collective-permute-start = (f32[1056,128]{1,0:T(8,128)S(1)}, f32[1056,128]{1,0:T(8,128)S(1)}, u32[]{:S(2)}, u32[]{:S(2)}) collective-permute-start(f32[1056,128]{1,0:T(8,128)S(1)} %given_first.1.mine_ref._), channel_id=1, source_target_pairs={{0,1},{1,0},{2,3},{3,2},{4,7},{5,6},{6,5},{7,4},{8,9},{9,8},{10,11... | collective-permute-start | bytes 1622024 | tf_op jit(solution)/shard_map/ppermute | solution.py:375
  19.6 3.4 %copy-start = (bf16[8192,512]{1,0:T(8,128)(2,1)S(1)}, bf16[8192,512]{1,0:T(8,128)(2,1)}, u32[]{:S(2)}) copy-start(bf16[8192,512]{1,0:T(8,128)(2,1)} %refs_0_.5) | copy-start | bytes 25165828
  23.0 27.2 %slice-start = ((s8[8388608]{0:T(1024)(128)(4,1)}), s8[4194304]{0:T(1024)(128)(4,1)S(1)}, s32[]{:S(2)}) async-start(s8[8388608]{0:T(1024)(128)(4,1)} %bitcast), calls=%async_computation.1 | async-start | bytes 8388608
  23.7 26.5 %slice-start.1 = ((s8[8388608]{0:T(1024)(128)(4,1)}), s8[4194304]{0:T(1024)(128)(4,1)S(1)}, s32[]{:S(2)}) async-start(s8[8388608]{0:T(1024)(128)(4,1)} %bitcast), calls=%async_computation.2 | async-start | bytes 8388608
  23.7 8.2 %collective-permute-start.3 = (f32[512,128]{1,0:T(8,128)S(1)}, f32[512,128]{1,0:T(8,128)S(1)}, u32[]{:S(2)}, u32[]{:S(2)}) collective-permute-start(f32[512,128]{1,0:T(8,128)S(1)} %get-tuple-element.20.mine_ref), channel_id=1, source_target_pairs={{0,1},{1,0},{2,3},{3,2},{4,7},{5,6},{6,5},{7,4},{8,9},{9,8},{10,11... | collective-permute-start | bytes 786440 | tf_op jit(solution)/shard_map/ppermute | solution.py:375
  27.8 13.2 %collective-permute-start.1 = (f32[544,128]{1,0:T(8,128)S(1)}, f32[544,128]{1,0:T(8,128)S(1)}, u32[]{:S(2)}, u32[]{:S(2)}) collective-permute-start(f32[544,128]{1,0:T(8,128)S(1)} %get-tuple-element.17.sent_ref), channel_id=1, source_target_pairs={{0,3},{1,2},{2,1},{3,0},{4,5},{5,4},{6,7},{7,6},{8,11},{9,10},{10,... | collective-permute-start | bytes 835592 | tf_op jit(solution)/shard_map/ppermute | solution.py:378
  31.9 9.1 %collective-permute-start.2 = (f32[512,128]{1,0:T(8,128)S(1)}, f32[512,128]{1,0:T(8,128)S(1)}, u32[]{:S(2)}, u32[]{:S(2)}) collective-permute-start(f32[512,128]{1,0:T(8,128)S(1)} %get-tuple-element.19), channel_id=1, source_target_pairs={{0,1},{1,0},{2,3},{3,2},{4,7},{5,6},{6,5},{7,4},{8,9},{9,8},{10,11... | collective-permute-start | bytes 786440 | tf_op jit(solution)/shard_map/ppermute | solution.py:375
  32.6 13.0 %collective-permute-start.4 = (f32[512,128]{1,0:T(8,128)S(1)}, f32[512,128]{1,0:T(8,128)S(1)}, u32[]{:S(2)}, u32[]{:S(2)}) collective-permute-start(f32[512,128]{1,0:T(8,128)S(1)} %get-tuple-element.22), channel_id=1, source_target_pairs={{0,3},{1,2},{2,1},{3,0},{4,5},{5,4},{6,7},{7,6},{8,11},{9,10},{10,... | collective-permute-start | bytes 786440 | tf_op jit(solution)/shard_map/ppermute | solution.py:378
  41.0 8.6 %collective-permute-start.6 = (f32[512,128]{1,0:T(8,128)S(1)}, f32[512,128]{1,0:T(8,128)S(1)}, u32[]{:S(2)}, u32[]{:S(2)}) collective-permute-start(f32[512,128]{1,0:T(8,128)S(1)} %added.2.refs_2_), channel_id=1, source_target_pairs={{0,3},{1,2},{2,1},{3,0},{4,5},{5,4},{6,7},{7,6},{8,11},{9,10},{10,... | collective-permute-start | bytes 786440 | tf_op jit(solution)/shard_map/ppermute | solution.py:378
  41.8 7.8 %collective-permute-start.5 = (f32[512,128]{1,0:T(8,128)S(1)}, f32[512,128]{1,0:T(8,128)S(1)}, u32[]{:S(2)}, u32[]{:S(2)}) collective-permute-start(f32[512,128]{1,0:T(8,128)S(1)} %added.2.refs_2_), channel_id=1, source_target_pairs={{0,1},{1,0},{2,3},{3,2},{4,7},{5,6},{6,5},{7,4},{8,9},{9,8},{10,11... | collective-permute-start | bytes 786440 | tf_op jit(solution)/shard_map/ppermute | solution.py:375
  45.6 10.5 %collective-permute-start.7 = (f32[512,128]{1,0:T(8,128)S(1)}, f32[512,128]{1,0:T(8,128)S(1)}, u32[]{:S(2)}, u32[]{:S(2)}) collective-permute-start(f32[512,128]{1,0:T(8,128)S(1)} %added.3.refs_3_), channel_id=1, source_target_pairs={{0,3},{1,2},{2,1},{3,0},{4,5},{5,4},{6,7},{7,6},{8,11},{9,10},{10,... | collective-permute-start | bytes 786440 | tf_op jit(solution)/shard_map/ppermute | solution.py:378
  48.2 8.8 %collective-permute-start.9 = (f32[512,128]{1,0:T(8,128)S(1)}, f32[512,128]{1,0:T(8,128)S(1)}, u32[]{:S(2)}, u32[]{:S(2)}) collective-permute-start(f32[512,128]{1,0:T(8,128)S(1)} %added.3.refs_3_), channel_id=1, source_target_pairs={{0,1},{1,0},{2,3},{3,2},{4,7},{5,6},{6,5},{7,4},{8,9},{9,8},{10,11... | collective-permute-start | bytes 786440 | tf_op jit(solution)/shard_map/ppermute | solution.py:375
  49.6 7.8 %collective-permute-start.10 = (f32[512,128]{1,0:T(8,128)S(1)}, f32[512,128]{1,0:T(8,128)S(1)}, u32[]{:S(2)}, u32[]{:S(2)}) collective-permute-start(f32[512,128]{1,0:T(8,128)S(1)} %in_order.2.refs_4_), channel_id=1, source_target_pairs={{0,1},{1,0},{2,3},{3,2},{4,7},{5,6},{6,5},{7,4},{8,9},{9,8},{10,11... | collective-permute-start | bytes 786440 | tf_op jit(solution)/shard_map/ppermute | solution.py:375
  56.1 6.4 %collective-permute-start.8 = (f32[512,128]{1,0:T(8,128)S(1)}, f32[512,128]{1,0:T(8,128)S(1)}, u32[]{:S(2)}, u32[]{:S(2)}) collective-permute-start(f32[512,128]{1,0:T(8,128)S(1)} %in_order.3.refs_2_), channel_id=1, source_target_pairs={{0,1},{1,0},{2,3},{3,2},{4,7},{5,6},{6,5},{7,4},{8,9},{9,8},{10,11... | collective-permute-start | bytes 786440 | tf_op jit(solution)/shard_map/ppermute | solution.py:375

commit v4 on v3

--- a/solution.py
+++ b/solution.py
@@ -383,14 +383,15 @@
     message = given_first(ahead, panel)
     got = swap_first(message)
     passing, staying = given_rest(emb, panel, block_rows, 1, message)
-    next_got, staying = swap_first(passing), swap_first(staying)
+    next_got = swap_first(passing)
     sent, own = zip(
         kept_products(emb, panel, got, message, block_rows, 0), kept_products(emb, panel, next_got, passing, block_rows, 1)
     )
     quarters = [swap_second(m) for m in sent]
+    staying = swap_first(in_order(staying, sent[1]))
     right = update_matrix(sent[0], quarters[0], panel)
 
-    totals = [added([own[0], quarters[0]], [staying]), added([own[1], staying, quarters[1]], [right])]
+    totals = [added([own[0], quarters[0]], []), added([own[1], staying, quarters[1]], [right])]
     near = [swap_second(t) for t in totals]
     theirs = [swap_first(t) for t in totals]
     last = count - 1

time: 64.4 us -> 63.3 us (0.983)
  waiting for transfers between devices: 14 us -> 11.9 us
  starting transfers between devices: 14.7 us -> 15.6 us
    ppermute x7, waiting for transfers between devices: 11.2 us -> 6.11 us  [swap_first(): return lax.ppermute(value, ('rows', 'cols'), first_pairs)]
    ppermute x4, waiting for transfers between devices: 2.79 us -> 5.78 us  [swap_second(): return lax.ppermute(value, ('rows', 'cols'), second_pairs)]
    ppermute x4, starting transfers between devices: 9.62 us -> 12.2 us  [swap_second(): return lax.ppermute(value, ('rows', 'cols'), second_pairs)]
    ppermute x7, starting transfers between devices: 5.08 us -> 3.43 us  [swap_first(): return lax.ppermute(value, ('rows', 'cols'), first_pairs)]
  transfers between devices with their start and end apart: 11 -> 11, of which waited for: 5 -> 7; matrix products, arithmetic and copies ran while one was open for 0% -> 0% of each run, Pallas kernels for 20% -> 20%
where the time goes in v4:
time: 63.3 us; the launch traced here: 63 us
  Pallas kernels  16.9 us (27%)
  starting transfers between devices  15.6 us (25%)
  blocking collectives  15 us (24%)
  waiting for transfers between devices  11.9 us (19%)
  local copies, waits for them, and re-layouts  3.48 us (5%)
    all_to_all x1, blocking collectives, per_device(): lax.all_to_all(mine, 'rows', 0, 0, tiled=True)  15 us
    ppermute x4, starting transfers between devices, swap_second(): return lax.ppermute(value, ('rows', 'cols'), second_pairs)  12.2 us
    pallas_call x3, Pallas kernels, update(): call(body, [jax.ShapeDtypeStruct((rows, width), F32)] + [pltpu.VMEM((8, 1...  8.58 us
    ppermute x7, waiting for transfers between devices, swap_first(): return lax.ppermute(value, ('rows', 'cols'), first_pairs)  6.11 us
    ppermute x4, waiting for transfers between devices, swap_second(): return lax.ppermute(value, ('rows', 'cols'), second_pairs)  5.78 us
    pallas_call x1, Pallas kernels, update_matrix(): call(body, pltpu.VMEM((6 * picks, width), BF16), [whole()] * 3, whole(),...  3.7 us
    ppermute x7, starting transfers between devices, swap_first(): return lax.ppermute(value, ('rows', 'cols'), first_pairs)  3.43 us
    unnamed x6, local copies, waits for them, and re-layouts  3.39 us
  transfers between devices with their start and end apart: 11, of which 7 were waited for; matrix products, arithmetic and copies ran while one was open for 0% of the time, Pallas kernels for 20%

profile of v4, /device:TPU:0, one launch (start us, length us, event | category | flops | bytes accessed | tf_op | source)
XLA Modules:
  0.0 63.0 jit_solution(10917361659032434556)
XLA Ops:
  0.0 1.8 %own_picks.1 = (f32[32,2,512]{2,1,0:T(2,128)S(1)}, bf16[2,1024,512]{2,1,0:T(8,128)(2,1)S(1)}) custom-call(s32[2,32]{1,0:T(2,128)} %picks_ref.1, bf16[8192,512]{1,0:T(8,128)(2,1)} %refs_0_.5), custom_call_target="tpu_custom_call" | custom-call | bytes 3000000 | tf_op jit(solution)/shard_map/own_picks/pallas_call | solution.py:122
  1.8 15.0 %all_to_all.5 = f32[32,2,512]{2,1,0:T(2,128)S(1)} all-to-all(f32[32,2,512]{2,1,0:T(2,128)S(1)} %get-tuple-element.15), channel_id=1, replica_groups=mesh['rows'=32,'cols'=4] {'rows'}, dimensions={0} | all-to-all | bytes 262144 | tf_op jit(solution)/shard_map/all_to_all | solution.py:381
  16.8 0.1 reshape.3.panel_ref
  16.9 0.7 %given_first.1.mine_ref._ = f32[1056,128]{1,0:T(8,128)S(1)} custom-call(bf16[2,1024,512]{2,1,0:T(8,128)(2,1)S(1)} %get-tuple-element.16.ahead_ref, f32[64,512]{1,0:T(8,128)S(1)} %reshape.3.panel_ref), custom_call_target="tpu_custom_call" | custom-call | bytes 3000000 | tf_op jit(solution)/shard_map/given_first/pallas_call | solution.py:163
  17.6 2.0 %collective-permute-start = (f32[1056,128]{1,0:T(8,128)S(1)}, f32[1056,128]{1,0:T(8,128)S(1)}, u32[]{:S(2)}, u32[]{:S(2)}) collective-permute-start(f32[1056,128]{1,0:T(8,128)S(1)} %given_first.1.mine_ref._), channel_id=1, source_target_pairs={{0,1},{1,0},{2,3},{3,2},{4,7},{5,6},{6,5},{7,4},{8,9},{9,8},{10,11... | collective-permute-start | bytes 1622024 | tf_op jit(solution)/shard_map/ppermute | solution.py:375
  19.6 0.0 copy-start
  19.6 3.4 %copy-done = bf16[8192,512]{1,0:T(8,128)(2,1)S(1)} copy-done((bf16[8192,512]{1,0:T(8,128)(2,1)S(1)}, bf16[8192,512]{1,0:T(8,128)(2,1)}, u32[]{:S(2)}) %copy-start) | copy-done | bytes 8388632
  23.0 0.0 slice-start
  23.0 0.7 %given_rest.1 = (f32[512,128]{1,0:T(8,128)S(1)}, f32[512,128]{1,0:T(8,128)S(1)}) custom-call(bf16[8192,512]{1,0:T(8,128)(2,1)S(1)} %copy-done, f32[64,512]{1,0:T(8,128)S(1)} %reshape.3.panel_ref, f32[1056,128]{1,0:T(8,128)S(1)} %given_first.1.mine_ref._), custom_call_target="tpu_custom_call" | custom-call | bytes 3000000 | tf_op jit(solution)/shard_map/given_rest/pallas_call | solution.py:183
  23.7 0.0 slice-start.1
  23.7 0.2 collective-permute-start.2
  23.9 3.2 %collective-permute-done.got_ref = f32[1056,128]{1,0:T(8,128)S(1)} collective-permute-done((f32[1056,128]{1,0:T(8,128)S(1)}, f32[1056,128]{1,0:T(8,128)S(1)}, u32[]{:S(2)}, u32[]{:S(2)}) %collective-permute-start) | collective-permute-done | bytes 540704 | tf_op jit(solution)/shard_map/ppermute | solution.py:375
  27.1 0.7 %kept_products.2 = (f32[544,128]{1,0:T(8,128)S(1)}, f32[512,128]{1,0:T(8,128)S(1)}) custom-call(bf16[8192,512]{1,0:T(8,128)(2,1)S(1)} %copy-done, f32[64,512]{1,0:T(8,128)S(1)} %reshape.3.panel_ref, f32[1056,128]{1,0:T(8,128)S(1)} %collective-permute-done.got_ref, f32[1056,128]{1,0:T(8,128)S(1)} %given_first.1.mine_ref._), custom_call_target="tpu_custom_call" | custom-call | bytes 3000000 | tf_op jit(solution)/shard_map/kept_products/pallas_call | solution.py:207
  27.8 4.1 %collective-permute-start.1 = (f32[544,128]{1,0:T(8,128)S(1)}, f32[544,128]{1,0:T(8,128)S(1)}, u32[]{:S(2)}, u32[]{:S(2)}) collective-permute-start(f32[544,128]{1,0:T(8,128)S(1)} %get-tuple-element.17.sent_ref), channel_id=1, source_target_pairs={{0,3},{1,2},{2,1},{3,0},{4,5},{5,4},{6,7},{7,6},{8,11},{9,10},{10,... | collective-permute-start | bytes 835592 | tf_op jit(solution)/shard_map/ppermute | solution.py:378
  31.9 0.0 collective-permute-done.2.got_ref
  31.9 0.7 %kept_products.3 = (f32[512,128]{1,0:T(8,128)S(1)}, f32[512,128]{1,0:T(8,128)S(1)}) custom-call(bf16[8192,512]{1,0:T(8,128)(2,1)S(1)} %copy-done, f32[64,512]{1,0:T(8,128)S(1)} %reshape.3.panel_ref, f32[512,128]{1,0:T(8,128)S(1)} %collective-permute-done.2.got_ref, f32[512,128]{1,0:T(8,128)S(1)} %get-tuple-element.19.mine_ref), custom_call_target="tpu_custom_call" | custom-call | bytes 3000000 | tf_op jit(solution)/shard_map/kept_products/pallas_call | solution.py:207
  32.6 0.1 collective-permute-start.3
  32.7 2.4 %collective-permute-start.4 = (f32[512,128]{1,0:T(8,128)S(1)}, f32[512,128]{1,0:T(8,128)S(1)}, u32[]{:S(2)}, u32[]{:S(2)}) collective-permute-start(f32[512,128]{1,0:T(8,128)S(1)} %get-tuple-element.21.refs_0_), channel_id=1, source_target_pairs={{0,3},{1,2},{2,1},{3,0},{4,5},{5,4},{6,7},{7,6},{8,11},{9,10},{10,... | collective-permute-start | bytes 786440 | tf_op jit(solution)/shard_map/ppermute | solution.py:378
  35.1 1.7 %collective-permute-done.1.got_ref.refs_1_ = f32[544,128]{1,0:T(8,128)S(1)} collective-permute-done((f32[544,128]{1,0:T(8,128)S(1)}, f32[544,128]{1,0:T(8,128)S(1)}, u32[]{:S(2)}, u32[]{:S(2)}) %collective-permute-start.1) | collective-permute-done | bytes 278560 | tf_op jit(solution)/shard_map/ppermute | solution.py:378
  36.9 3.8 %collective-permute-start.6 = (f32[512,128]{1,0:T(8,128)S(1)}, f32[512,128]{1,0:T(8,128)S(1)}, u32[]{:S(2)}, u32[]{:S(2)}) collective-permute-start(f32[512,128]{1,0:T(8,128)S(1)} %added.2.refs_2_), channel_id=1, source_target_pairs={{0,3},{1,2},{2,1},{3,0},{4,5},{5,4},{6,7},{7,6},{8,11},{9,10},{10,... | collective-permute-start | bytes 786440 | tf_op jit(solution)/shard_map/ppermute | solution.py:378
  40.6 0.0 collective-permute-start.5
  40.6 3.7 %update_matrix.1.refs_3_.refs_1_ = bf16[384,512]{1,0:T(8,128)(2,1)S(1)} custom-call(f32[544,128]{1,0:T(8,128)S(1)} %get-tuple-element.17.sent_ref, f32[544,128]{1,0:T(8,128)S(1)} %collective-permute-done.1.got_ref.refs_1_, f32[64,512]{1,0:T(8,128)S(1)} %reshape.3.panel_ref), custom_call_target="tpu_custom_call" | custom-call | bytes 3000000 | tf_op jit(solution)/shard_map/update_matrix/pallas_call | solution.py:295
  44.4 0.0 collective-permute-done.3.refs_1_
  44.4 0.0 collective-permute-done.4.refs_2_
  44.4 1.8 %collective-permute-start.7 = (f32[512,128]{1,0:T(8,128)S(1)}, f32[512,128]{1,0:T(8,128)S(1)}, u32[]{:S(2)}, u32[]{:S(2)}) collective-permute-start(f32[512,128]{1,0:T(8,128)S(1)} %added.3.refs_3_), channel_id=1, source_target_pairs={{0,3},{1,2},{2,1},{3,0},{4,5},{5,4},{6,7},{7,6},{8,11},{9,10},{10,... | collective-permute-start | bytes 786440 | tf_op jit(solution)/shard_map/ppermute | solution.py:378
  46.3 0.3 collective-permute-start.9
  46.6 2.1 %collective-permute-done.6.refs_1_ = f32[512,128]{1,0:T(8,128)S(1)} collective-permute-done((f32[512,128]{1,0:T(8,128)S(1)}, f32[512,128]{1,0:T(8,128)S(1)}, u32[]{:S(2)}, u32[]{:S(2)}) %collective-permute-start.6) | collective-permute-done | bytes 262176 | tf_op jit(solution)/shard_map/ppermute | solution.py:378
  48.7 1.2 %collective-permute-done.5.refs_0_.refs_3_ = f32[512,128]{1,0:T(8,128)S(1)} collective-permute-done((f32[512,128]{1,0:T(8,128)S(1)}, f32[512,128]{1,0:T(8,128)S(1)}, u32[]{:S(2)}, u32[]{:S(2)}) %collective-permute-start.5) | collective-permute-done | bytes 262176 | tf_op jit(solution)/shard_map/ppermute | solution.py:375
  49.9 0.0 collective-permute-start.10
  49.9 0.0 slice-done
  49.9 0.0 slice-done.1
  49.9 3.1 %update_near.1 = (f32[8192,512]{1,0:T(8,128)}, f32[8,128]{1,0:T(8,128)S(1)}) custom-call(bf16[8192,512]{1,0:T(8,128)(2,1)S(1)} %bitcast.1, bf16[384,512]{1,0:T(8,128)(2,1)S(1)} %update_matrix.1.refs_3_.refs_1_, f32[512,128]{1,0:T(8,128)S(1)} %added.2.refs_2_, f32[512,128]{1,0:T(8,128)S(1)} %added.3.refs_3_, f32[512,128]{1,0:T(8,128)S(1)} %in_order.4.refs_4_), custom_call_target="tpu_custom_call" | custom-call | bytes 3000000 | tf_op jit(solution)/shard_map/update_near/pallas_call | solution.py:355
  53.0 1.9 %collective-permute-done.7.refs_1_ = f32[512,128]{1,0:T(8,128)S(1)} collective-permute-done((f32[512,128]{1,0:T(8,128)S(1)}, f32[512,128]{1,0:T(8,128)S(1)}, u32[]{:S(2)}, u32[]{:S(2)}) %collective-permute-start.7) | collective-permute-done | bytes 262176 | tf_op jit(solution)/shard_map/ppermute | solution.py:378
  55.0 0.8 %collective-permute-start.8 = (f32[512,128]{1,0:T(8,128)S(1)}, f32[512,128]{1,0:T(8,128)S(1)}, u32[]{:S(2)}, u32[]{:S(2)}) collective-permute-start(f32[512,128]{1,0:T(8,128)S(1)} %in_order.5.refs_2_), channel_id=1, source_target_pairs={{0,1},{1,0},{2,3},{3,2},{4,7},{5,6},{6,5},{7,4},{8,9},{9,8},{10,11... | collective-permute-start | bytes 786440 | tf_op jit(solution)/shard_map/ppermute | solution.py:375
  55.8 0.0 collective-permute-done.9.refs_4_
  55.8 0.5 collective-permute-done.10.refs_5_
  56.3 3.8 %update_far.1.refs_3_ = f32[8192,512]{1,0:T(8,128)} custom-call(bf16[8192,512]{1,0:T(8,128)(2,1)S(1)} %bitcast.1, bf16[384,512]{1,0:T(8,128)(2,1)S(1)} %update_matrix.1.refs_3_.refs_1_, f32[512,128]{1,0:T(8,128)S(1)} %in_order.5.refs_2_, f32[512,128]{1,0:T(8,128)S(1)} %collective-permute-done.5.refs_0_.refs_3_, ...), custom_call_target="tpu_custom_call", output_to_operand_aliasing={{}: (6, {})} | custom-call | bytes 3000000 | tf_op jit(solution)/shard_map/update_far/pallas_call | solution.py:355
  60.0 1.3 %collective-permute-done.8.refs_2_ = f32[512,128]{1,0:T(8,128)S(1)} collective-permute-done((f32[512,128]{1,0:T(8,128)S(1)}, f32[512,128]{1,0:T(8,128)S(1)}, u32[]{:S(2)}, u32[]{:S(2)}) %collective-permute-start.8) | collective-permute-done | bytes 262176 | tf_op jit(solution)/shard_map/ppermute | solution.py:375
  61.3 1.7 %update_last.1 = f32[8192,512]{1,0:T(8,128)} custom-call(bf16[8192,512]{1,0:T(8,128)(2,1)S(1)} %bitcast.1, bf16[384,512]{1,0:T(8,128)(2,1)S(1)} %update_matrix.1.refs_3_.refs_1_, f32[512,128]{1,0:T(8,128)S(1)} %collective-permute-done.8.refs_2_, f32[8192,512]{1,0:T(8,128)} %update_far.1.refs_3_), custom_call_target="tpu_custom_call", output_to_operand_aliasing={{}: (3, {})} | custom-call | bytes 3000000 | tf_op jit(solution)/shard_map/update_last/pallas_call | solution.py:355
  (6 shorter events, 0.1 us)
Async XLA Ops:
  17.6 9.4 %collective-permute-start = (f32[1056,128]{1,0:T(8,128)S(1)}, f32[1056,128]{1,0:T(8,128)S(1)}, u32[]{:S(2)}, u32[]{:S(2)}) collective-permute-start(f32[1056,128]{1,0:T(8,128)S(1)} %given_first.1.mine_ref._), channel_id=1, source_target_pairs={{0,1},{1,0},{2,3},{3,2},{4,7},{5,6},{6,5},{7,4},{8,9},{9,8},{10,11... | collective-permute-start | bytes 1622024 | tf_op jit(solution)/shard_map/ppermute | solution.py:375
  19.6 3.4 %copy-start = (bf16[8192,512]{1,0:T(8,128)(2,1)S(1)}, bf16[8192,512]{1,0:T(8,128)(2,1)}, u32[]{:S(2)}) copy-start(bf16[8192,512]{1,0:T(8,128)(2,1)} %refs_0_.5) | copy-start | bytes 25165828
  23.0 26.9 %slice-start = ((s8[8388608]{0:T(1024)(128)(4,1)}), s8[4194304]{0:T(1024)(128)(4,1)S(1)}, s32[]{:S(2)}) async-start(s8[8388608]{0:T(1024)(128)(4,1)} %bitcast), calls=%async_computation.1 | async-start | bytes 8388608
  23.7 26.2 %slice-start.1 = ((s8[8388608]{0:T(1024)(128)(4,1)}), s8[4194304]{0:T(1024)(128)(4,1)S(1)}, s32[]{:S(2)}) async-start(s8[8388608]{0:T(1024)(128)(4,1)} %bitcast), calls=%async_computation.2 | async-start | bytes 8388608
  23.7 8.2 %collective-permute-start.2 = (f32[512,128]{1,0:T(8,128)S(1)}, f32[512,128]{1,0:T(8,128)S(1)}, u32[]{:S(2)}, u32[]{:S(2)}) collective-permute-start(f32[512,128]{1,0:T(8,128)S(1)} %get-tuple-element.19.mine_ref), channel_id=1, source_target_pairs={{0,1},{1,0},{2,3},{3,2},{4,7},{5,6},{6,5},{7,4},{8,9},{9,8},{10,11... | collective-permute-start | bytes 786440 | tf_op jit(solution)/shard_map/ppermute | solution.py:375
  27.8 9.1 %collective-permute-start.1 = (f32[544,128]{1,0:T(8,128)S(1)}, f32[544,128]{1,0:T(8,128)S(1)}, u32[]{:S(2)}, u32[]{:S(2)}) collective-permute-start(f32[544,128]{1,0:T(8,128)S(1)} %get-tuple-element.17.sent_ref), channel_id=1, source_target_pairs={{0,3},{1,2},{2,1},{3,0},{4,5},{5,4},{6,7},{7,6},{8,11},{9,10},{10,... | collective-permute-start | bytes 835592 | tf_op jit(solution)/shard_map/ppermute | solution.py:378
  32.6 11.8 %collective-permute-start.3 = (f32[512,128]{1,0:T(8,128)S(1)}, f32[512,128]{1,0:T(8,128)S(1)}, u32[]{:S(2)}, u32[]{:S(2)}) collective-permute-start(f32[512,128]{1,0:T(8,128)S(1)} %in_order.3), channel_id=1, source_target_pairs={{0,1},{1,0},{2,3},{3,2},{4,7},{5,6},{6,5},{7,4},{8,9},{9,8},{10,11... | collective-permute-start | bytes 786440 | tf_op jit(solution)/shard_map/ppermute | solution.py:375
  32.7 11.7 %collective-permute-start.4 = (f32[512,128]{1,0:T(8,128)S(1)}, f32[512,128]{1,0:T(8,128)S(1)}, u32[]{:S(2)}, u32[]{:S(2)}) collective-permute-start(f32[512,128]{1,0:T(8,128)S(1)} %get-tuple-element.21.refs_0_), channel_id=1, source_target_pairs={{0,3},{1,2},{2,1},{3,0},{4,5},{5,4},{6,7},{7,6},{8,11},{9,10},{10,... | collective-permute-start | bytes 786440 | tf_op jit(solution)/shard_map/ppermute | solution.py:378
  36.9 11.8 %collective-permute-start.6 = (f32[512,128]{1,0:T(8,128)S(1)}, f32[512,128]{1,0:T(8,128)S(1)}, u32[]{:S(2)}, u32[]{:S(2)}) collective-permute-start(f32[512,128]{1,0:T(8,128)S(1)} %added.2.refs_2_), channel_id=1, source_target_pairs={{0,3},{1,2},{2,1},{3,0},{4,5},{5,4},{6,7},{7,6},{8,11},{9,10},{10,... | collective-permute-start | bytes 786440 | tf_op jit(solution)/shard_map/ppermute | solution.py:378
  40.6 9.2 %collective-permute-start.5 = (f32[512,128]{1,0:T(8,128)S(1)}, f32[512,128]{1,0:T(8,128)S(1)}, u32[]{:S(2)}, u32[]{:S(2)}) collective-permute-start(f32[512,128]{1,0:T(8,128)S(1)} %added.2.refs_2_), channel_id=1, source_target_pairs={{0,1},{1,0},{2,3},{3,2},{4,7},{5,6},{6,5},{7,4},{8,9},{9,8},{10,11... | collective-permute-start | bytes 786440 | tf_op jit(solution)/shard_map/ppermute | solution.py:375
  44.4 10.5 %collective-permute-start.7 = (f32[512,128]{1,0:T(8,128)S(1)}, f32[512,128]{1,0:T(8,128)S(1)}, u32[]{:S(2)}, u32[]{:S(2)}) collective-permute-start(f32[512,128]{1,0:T(8,128)S(1)} %added.3.refs_3_), channel_id=1, source_target_pairs={{0,3},{1,2},{2,1},{3,0},{4,5},{5,4},{6,7},{7,6},{8,11},{9,10},{10,... | collective-permute-start | bytes 786440 | tf_op jit(solution)/shard_map/ppermute | solution.py:378
  46.3 9.5 %collective-permute-start.9 = (f32[512,128]{1,0:T(8,128)S(1)}, f32[512,128]{1,0:T(8,128)S(1)}, u32[]{:S(2)}, u32[]{:S(2)}) collective-permute-start(f32[512,128]{1,0:T(8,128)S(1)} %added.3.refs_3_), channel_id=1, source_target_pairs={{0,1},{1,0},{2,3},{3,2},{4,7},{5,6},{6,5},{7,4},{8,9},{9,8},{10,11... | collective-permute-start | bytes 786440 | tf_op jit(solution)/shard_map/ppermute | solution.py:375
  49.9 6.4 %collective-permute-start.10 = (f32[512,128]{1,0:T(8,128)S(1)}, f32[512,128]{1,0:T(8,128)S(1)}, u32[]{:S(2)}, u32[]{:S(2)}) collective-permute-start(f32[512,128]{1,0:T(8,128)S(1)} %in_order.4.refs_4_), channel_id=1, source_target_pairs={{0,1},{1,0},{2,3},{3,2},{4,7},{5,6},{6,5},{7,4},{8,9},{9,8},{10,11... | collective-permute-start | bytes 786440 | tf_op jit(solution)/shard_map/ppermute | solution.py:375
  55.0 6.4 %collective-permute-start.8 = (f32[512,128]{1,0:T(8,128)S(1)}, f32[512,128]{1,0:T(8,128)S(1)}, u32[]{:S(2)}, u32[]{:S(2)}) collective-permute-start(f32[512,128]{1,0:T(8,128)S(1)} %in_order.5.refs_2_), channel_id=1, source_target_pairs={{0,1},{1,0},{2,3},{3,2},{4,7},{5,6},{6,5},{7,4},{8,9},{9,8},{10,11... | collective-permute-start | bytes 786440 | tf_op jit(solution)/shard_map/ppermute | solution.py:375

commit v5 on v4

--- a/solution.py
+++ b/solution.py
@@ -189,28 +189,37 @@
     )(emb, in_vmem(panel), after)
 
 
-def kept_products(emb, panel, got, message, block_rows, k):
+def passed_products(emb, panel, got, message, block_rows, k):
     picks = panel.shape[0]
     size = CHUNKS[k]
     extra = picks // 2 if k == 0 else 0
 
-    def body(emb_ref, panel_ref, got_ref, mine_ref, out_ref, own_ref):
+    def body(emb_ref, panel_ref, got_ref, mine_ref, out_ref):
         half, quarter, _ = kept()
         paired = paired_panel(panel_ref[...])
         start = block_start(half, 1 - quarter, block_rows, k)
         out_ref[:size, :] = quarter_products(emb_ref, start, size, paired) + got_ref[:size, :]
         if extra:
             out_ref[size:, :] = got_ref[2 * size :, :] + mine_ref[2 * size :, :]
-        own = quarter_products(emb_ref, block_start(half, quarter, block_rows, k), size, paired)
-        own_ref[...] = own + got_ref[size : 2 * size, :] if extra else own
-
-    return call(
-        body,
-        [pltpu.VMEM((size + extra, 2 * picks), F32), pltpu.VMEM((size, 2 * picks), F32)],
-        [whole()] * 4,
-        [whole()] * 2,
-        name="kept_products",
+
+    return call(
+        body, pltpu.VMEM((size + extra, 2 * picks), F32), [whole()] * 4, whole(), name="passed_products"
     )(emb, in_vmem(panel), in_vmem(got), in_vmem(message))
+
+
+def own_products(emb, panel, got, block_rows, k, after):
+    picks = panel.shape[0]
+    size = CHUNKS[k]
+
+    def body(emb_ref, panel_ref, got_ref, _, out_ref):
+        half, quarter, _ = kept()
+        paired = paired_panel(panel_ref[...])
+        mine = quarter_products(emb_ref, block_start(half, quarter, block_rows, k), size, paired)
+        out_ref[...] = mine + got_ref[size : 2 * size, :] if k == 0 else mine
+
+    return call(
+        body, pltpu.VMEM((size, 2 * picks), F32), [whole()] * 3 + [anywhere()], whole(), name="own_products"
+    )(emb, in_vmem(panel), in_vmem(got), after)
 
 
 def added(parts, after):
@@ -260,10 +269,10 @@
     return jnp.concatenate([total[:, :picks], total[:, picks:]], axis=0)
 
 
-def inverted(matrix):
+def pivoted(matrix, first_pivot, last_pivot):
     lane = lax.broadcasted_iota(jnp.int32, matrix.shape, 1)
     line = lax.broadcasted_iota(jnp.int32, matrix.shape, 0)
-    for k in range(0, matrix.shape[0], 2):
+    for k in range(first_pivot, last_pivot, 2):
         first = jnp.broadcast_to(matrix[:, k : k + 1], matrix.shape)
         second = jnp.broadcast_to(matrix[:, k + 1 : k + 2], matrix.shape)
         a, b, d = first[k : k + 1], second[k : k + 1], second[k + 1 : k + 2]
@@ -279,12 +288,23 @@
     return matrix
 
 
-def update_matrix(sent, got, panel):
+def first_pivots(sent, got):
+    picks = sent.shape[1] // 2
+
+    def body(sent_ref, got_ref, out_ref):
+        out_ref[...] = pivoted(gram_of(sent_ref, got_ref), 0, picks // 2)
+
+    return call(body, pltpu.VMEM((picks, picks), F32), [whole()] * 2, whole(), name="first_pivots")(
+        in_vmem(sent), in_vmem(got)
+    )
+
+
+def update_matrix(sent, got, halfway, panel):
     picks, width = panel.shape
 
-    def body(sent_ref, got_ref, panel_ref, out_ref):
+    def body(sent_ref, got_ref, halfway_ref, panel_ref, out_ref):
         gram = gram_of(sent_ref, got_ref)
-        inverse = inverted(gram)
+        inverse = pivoted(halfway_ref[...], picks // 2, picks)
         lane = lax.broadcasted_iota(jnp.int32, gram.shape, 1)
         line = lax.broadcasted_iota(jnp.int32, gram.shape, 0)
         eye = jnp.where(lane == line, 1.0, 0.0)
@@ -292,8 +312,8 @@
         high, middle, low = split(dot_full(inverse, panel_ref[...]))
         out_ref[...] = jnp.concatenate([high, high, high, low, middle, middle], axis=0)
 
-    return call(body, pltpu.VMEM((6 * picks, width), BF16), [whole()] * 3, whole(), name="update_matrix")(
-        in_vmem(sent), in_vmem(got), in_vmem(panel)
+    return call(body, pltpu.VMEM((6 * picks, width), BF16), [whole()] * 4, whole(), name="update_matrix")(
+        in_vmem(sent), in_vmem(got), in_vmem(halfway), in_vmem(panel)
     )
 
 
@@ -384,14 +404,17 @@
     got = swap_first(message)
     passing, staying = given_rest(emb, panel, block_rows, 1, message)
     next_got = swap_first(passing)
-    sent, own = zip(
-        kept_products(emb, panel, got, message, block_rows, 0), kept_products(emb, panel, next_got, passing, block_rows, 1)
-    )
+    sent = [
+        passed_products(emb, panel, got, message, block_rows, 0),
+        passed_products(emb, panel, next_got, passing, block_rows, 1),
+    ]
+    own = [own_products(emb, panel, g, block_rows, k, sent[k]) for k, g in enumerate((got, next_got))]
+    staying = swap_first(in_order(staying, own[1]))
     quarters = [swap_second(m) for m in sent]
-    staying = swap_first(in_order(staying, sent[1]))
-    right = update_matrix(sent[0], quarters[0], panel)
-
-    totals = [added([own[0], quarters[0]], []), added([own[1], staying, quarters[1]], [right])]
+    halfway = first_pivots(sent[0], quarters[0])
+    right = update_matrix(sent[0], quarters[0], halfway, panel)
+
+    totals = [added([own[0], quarters[0]], []), added([own[1], staying, quarters[1]], [halfway])]
     near = [swap_second(t) for t in totals]
     theirs = [swap_first(t) for t in totals]
     last = count - 1

time: 63.3 us -> 63.2 us (level)
  waiting for transfers between devices: 11.9 us -> 9.85 us
  starting transfers between devices: 15.6 us -> 16.7 us
    ppermute x4, waiting for transfers between devices: 5.78 us -> 3.88 us  [swap_second(): return lax.ppermute(value, ('rows', 'cols'), second_pairs)]
    ppermute x4, starting transfers between devices: 12.2 us -> 13.1 us  [swap_second(): return lax.ppermute(value, ('rows', 'cols'), second_pairs)]
    pallas_call x3 -> x6, Pallas kernels: 5.07 us -> 5.4 us  [the longest x1 2.14 us: update_matrix(): call(body, pltpu.VMEM((6 * picks, width), BF16), [whole()] * 4, whole(),...]
  transfers between devices with their start and end apart: 11 -> 11, of which waited for: 7 -> 8; matrix products, arithmetic and copies ran while one was open for 0% -> 0% of each run, Pallas kernels for 20% -> 21%
where the time goes in v5:
time: 63.2 us; the launch traced here: 62.6 us
  Pallas kernels  17.2 us (27%)
  starting transfers between devices  16.7 us (26%)
  blocking collectives  15 us (24%)
  waiting for transfers between devices  9.85 us (16%)
  local copies, waits for them, and re-layouts  3.49 us (6%)
    all_to_all x1, blocking collectives, per_device(): lax.all_to_all(mine, 'rows', 0, 0, tiled=True)  15 us
    ppermute x4, starting transfers between devices, swap_second(): return lax.ppermute(value, ('rows', 'cols'), second_pairs)  13.1 us
    pallas_call x3, Pallas kernels, update(): call(body, [jax.ShapeDtypeStruct((rows, width), F32)] + [pltpu.VMEM((8, 1...  8.57 us
    ppermute x7, waiting for transfers between devices, swap_first(): return lax.ppermute(value, ('rows', 'cols'), first_pairs)  5.96 us
    ppermute x4, waiting for transfers between devices, swap_second(): return lax.ppermute(value, ('rows', 'cols'), second_pairs)  3.88 us
    ppermute x7, starting transfers between devices, swap_first(): return lax.ppermute(value, ('rows', 'cols'), first_pairs)  3.61 us
    unnamed x6, local copies, waits for them, and re-layouts  3.4 us
    pallas_call x1, Pallas kernels, update_matrix(): call(body, pltpu.VMEM((6 * picks, width), BF16), [whole()] * 4, whole(),...  2.14 us
  transfers between devices with their start and end apart: 11, of which 8 were waited for; matrix products, arithmetic and copies ran while one was open for 0% of the time, Pallas kernels for 21%

profile of v5, /device:TPU:0, one launch (start us, length us, event | category | flops | bytes accessed | tf_op | source)
XLA Modules:
  0.0 62.6 jit_solution(5400092686937265510)
XLA Ops:
  0.0 1.8 %own_picks.1 = (f32[32,2,512]{2,1,0:T(2,128)S(1)}, bf16[2,1024,512]{2,1,0:T(8,128)(2,1)S(1)}) custom-call(s32[2,32]{1,0:T(2,128)} %picks_ref.1, bf16[8192,512]{1,0:T(8,128)(2,1)} %refs_0_.5), custom_call_target="tpu_custom_call" | custom-call | bytes 3000000 | tf_op jit(solution)/shard_map/own_picks/pallas_call | solution.py:122
  1.8 15.0 %all_to_all.5 = f32[32,2,512]{2,1,0:T(2,128)S(1)} all-to-all(f32[32,2,512]{2,1,0:T(2,128)S(1)} %get-tuple-element.11), channel_id=1, replica_groups=mesh['rows'=32,'cols'=4] {'rows'}, dimensions={0} | all-to-all | bytes 262144 | tf_op jit(solution)/shard_map/all_to_all | solution.py:401
  16.8 0.1 reshape.3.panel_ref
  16.9 0.7 %given_first.1.mine_ref._ = f32[1056,128]{1,0:T(8,128)S(1)} custom-call(bf16[2,1024,512]{2,1,0:T(8,128)(2,1)S(1)} %get-tuple-element.12.ahead_ref, f32[64,512]{1,0:T(8,128)S(1)} %reshape.3.panel_ref), custom_call_target="tpu_custom_call" | custom-call | bytes 3000000 | tf_op jit(solution)/shard_map/given_first/pallas_call | solution.py:163
  17.6 2.0 %collective-permute-start = (f32[1056,128]{1,0:T(8,128)S(1)}, f32[1056,128]{1,0:T(8,128)S(1)}, u32[]{:S(2)}, u32[]{:S(2)}) collective-permute-start(f32[1056,128]{1,0:T(8,128)S(1)} %given_first.1.mine_ref._), channel_id=1, source_target_pairs={{0,1},{1,0},{2,3},{3,2},{4,7},{5,6},{6,5},{7,4},{8,9},{9,8},{10,11... | collective-permute-start | bytes 1622024 | tf_op jit(solution)/shard_map/ppermute | solution.py:395
  19.6 0.0 copy-start
  19.6 3.4 %copy-done = bf16[8192,512]{1,0:T(8,128)(2,1)S(1)} copy-done((bf16[8192,512]{1,0:T(8,128)(2,1)S(1)}, bf16[8192,512]{1,0:T(8,128)(2,1)}, u32[]{:S(2)}) %copy-start) | copy-done | bytes 8388632
  23.0 0.7 %given_rest.1 = (f32[512,128]{1,0:T(8,128)S(1)}, f32[512,128]{1,0:T(8,128)S(1)}) custom-call(bf16[8192,512]{1,0:T(8,128)(2,1)S(1)} %copy-done, f32[64,512]{1,0:T(8,128)S(1)} %reshape.3.panel_ref, f32[1056,128]{1,0:T(8,128)S(1)} %given_first.1.mine_ref._), custom_call_target="tpu_custom_call" | custom-call | bytes 3000000 | tf_op jit(solution)/shard_map/given_rest/pallas_call | solution.py:183
  23.7 0.0 slice-start
  23.7 0.2 collective-permute-start.2
  23.9 3.2 %collective-permute-done.got_ref = f32[1056,128]{1,0:T(8,128)S(1)} collective-permute-done((f32[1056,128]{1,0:T(8,128)S(1)}, f32[1056,128]{1,0:T(8,128)S(1)}, u32[]{:S(2)}, u32[]{:S(2)}) %collective-permute-start) | collective-permute-done | bytes 540704 | tf_op jit(solution)/shard_map/ppermute | solution.py:395
  27.1 0.4 passed_products.2.sent_ref._
  27.5 0.0 slice-start.1
  27.5 4.1 %collective-permute-start.1 = (f32[544,128]{1,0:T(8,128)S(1)}, f32[544,128]{1,0:T(8,128)S(1)}, u32[]{:S(2)}, u32[]{:S(2)}) collective-permute-start(f32[544,128]{1,0:T(8,128)S(1)} %passed_products.2.sent_ref._), channel_id=1, source_target_pairs={{0,3},{1,2},{2,1},{3,0},{4,5},{5,4},{6,7},{7,6},{8,11},{9,10},{10,... | collective-permute-start | bytes 835592 | tf_op jit(solution)/shard_map/ppermute | solution.py:398
  31.6 0.0 collective-permute-done.2.got_ref
  31.6 0.4 passed_products.3._
  32.0 0.4 own_products.3.refs_0_
  32.5 0.3 collective-permute-start.3
  32.7 2.5 %collective-permute-start.4 = (f32[512,128]{1,0:T(8,128)S(1)}, f32[512,128]{1,0:T(8,128)S(1)}, u32[]{:S(2)}, u32[]{:S(2)}) collective-permute-start(f32[512,128]{1,0:T(8,128)S(1)} %passed_products.3._), channel_id=1, source_target_pairs={{0,3},{1,2},{2,1},{3,0},{4,5},{5,4},{6,7},{7,6},{8,11},{9,10},{10,... | collective-permute-start | bytes 786440 | tf_op jit(solution)/shard_map/ppermute | solution.py:398
  35.2 0.0 slice-done
  35.2 0.0 slice-done.1
  35.3 0.4 own_products.2.refs_0_
  35.7 0.5 collective-permute-done.1.got_ref.refs_1_
  36.2 3.8 %collective-permute-start.6 = (f32[512,128]{1,0:T(8,128)S(1)}, f32[512,128]{1,0:T(8,128)S(1)}, u32[]{:S(2)}, u32[]{:S(2)}) collective-permute-start(f32[512,128]{1,0:T(8,128)S(1)} %added.2.refs_2_), channel_id=1, source_target_pairs={{0,3},{1,2},{2,1},{3,0},{4,5},{5,4},{6,7},{7,6},{8,11},{9,10},{10,... | collective-permute-start | bytes 786440 | tf_op jit(solution)/shard_map/ppermute | solution.py:398
  40.0 0.0 collective-permute-start.5
  40.0 1.6 %first_pivots.1.halfway_ref.refs_3_ = f32[64,64]{1,0:T(8,128)S(1)} custom-call(f32[544,128]{1,0:T(8,128)S(1)} %passed_products.2.sent_ref._, f32[544,128]{1,0:T(8,128)S(1)} %collective-permute-done.1.got_ref.refs_1_), custom_call_target="tpu_custom_call" | custom-call | bytes 3000000 | tf_op jit(solution)/shard_map/first_pivots/pallas_call | solution.py:297
  41.6 0.0 collective-permute-done.3.refs_1_
  41.6 1.5 %collective-permute-done.4.refs_2_ = f32[512,128]{1,0:T(8,128)S(1)} collective-permute-done((f32[512,128]{1,0:T(8,128)S(1)}, f32[512,128]{1,0:T(8,128)S(1)}, u32[]{:S(2)}, u32[]{:S(2)}) %collective-permute-start.4) | collective-permute-done | bytes 262176 | tf_op jit(solution)/shard_map/ppermute | solution.py:398
  43.1 2.7 %collective-permute-start.7 = (f32[512,128]{1,0:T(8,128)S(1)}, f32[512,128]{1,0:T(8,128)S(1)}, u32[]{:S(2)}, u32[]{:S(2)}) collective-permute-start(f32[512,128]{1,0:T(8,128)S(1)} %added.3.refs_3_), channel_id=1, source_target_pairs={{0,3},{1,2},{2,1},{3,0},{4,5},{5,4},{6,7},{7,6},{8,11},{9,10},{10,... | collective-permute-start | bytes 786440 | tf_op jit(solution)/shard_map/ppermute | solution.py:398
  45.8 0.0 collective-permute-start.9
  45.8 2.1 %update_matrix.1.refs_1_ = bf16[384,512]{1,0:T(8,128)(2,1)S(1)} custom-call(f32[544,128]{1,0:T(8,128)S(1)} %passed_products.2.sent_ref._, f32[544,128]{1,0:T(8,128)S(1)} %collective-permute-done.1.got_ref.refs_1_, f32[64,64]{1,0:T(8,128)S(1)} %first_pivots.1.halfway_ref.refs_3_, f32[64,512]{1,0:T(8,128)S(1)} %reshape.3.panel_ref), custom_call_target="tpu_custom_call" | custom-call | bytes 3000000 | tf_op jit(solution)/shard_map/update_matrix/pallas_call | solution.py:315
  47.9 0.8 %collective-permute-done.6.refs_1_ = f32[512,128]{1,0:T(8,128)S(1)} collective-permute-done((f32[512,128]{1,0:T(8,128)S(1)}, f32[512,128]{1,0:T(8,128)S(1)}, u32[]{:S(2)}, u32[]{:S(2)}) %collective-permute-start.6) | collective-permute-done | bytes 262176 | tf_op jit(solution)/shard_map/ppermute | solution.py:398
  48.7 0.5 collective-permute-done.5.refs_0_.refs_3_
  49.2 0.9 %collective-permute-start.10 = (f32[512,128]{1,0:T(8,128)S(1)}, f32[512,128]{1,0:T(8,128)S(1)}, u32[]{:S(2)}, u32[]{:S(2)}) collective-permute-start(f32[512,128]{1,0:T(8,128)S(1)} %in_order.4.refs_4_), channel_id=1, source_target_pairs={{0,1},{1,0},{2,3},{3,2},{4,7},{5,6},{6,5},{7,4},{8,9},{9,8},{10,11... | collective-permute-start | bytes 786440 | tf_op jit(solution)/shard_map/ppermute | solution.py:395
  50.1 3.1 %update_near.1 = (f32[8192,512]{1,0:T(8,128)}, f32[8,128]{1,0:T(8,128)S(1)}) custom-call(bf16[8192,512]{1,0:T(8,128)(2,1)S(1)} %bitcast.1, bf16[384,512]{1,0:T(8,128)(2,1)S(1)} %update_matrix.1.refs_1_, f32[512,128]{1,0:T(8,128)S(1)} %added.2.refs_2_, f32[512,128]{1,0:T(8,128)S(1)} %added.3.refs_3_, f32[512,128]{1,0:T(8,128)S(1)} %in_order.4.refs_4_), custom_call_target="tpu_custom_call" | custom-call | bytes 3000000 | tf_op jit(solution)/shard_map/update_near/pallas_call | solution.py:375
  53.2 1.1 %collective-permute-done.7.refs_1_ = f32[512,128]{1,0:T(8,128)S(1)} collective-permute-done((f32[512,128]{1,0:T(8,128)S(1)}, f32[512,128]{1,0:T(8,128)S(1)}, u32[]{:S(2)}, u32[]{:S(2)}) %collective-permute-start.7) | collective-permute-done | bytes 262176 | tf_op jit(solution)/shard_map/ppermute | solution.py:398
  54.3 0.3 collective-permute-start.8
  54.6 0.0 collective-permute-done.9.refs_4_
  54.6 1.1 %collective-permute-done.10.refs_5_ = f32[512,128]{1,0:T(8,128)S(1)} collective-permute-done((f32[512,128]{1,0:T(8,128)S(1)}, f32[512,128]{1,0:T(8,128)S(1)}, u32[]{:S(2)}, u32[]{:S(2)}) %collective-permute-start.10) | collective-permute-done | bytes 262176 | tf_op jit(solution)/shard_map/ppermute | solution.py:395
  55.8 3.8 %update_far.1.refs_3_ = f32[8192,512]{1,0:T(8,128)} custom-call(bf16[8192,512]{1,0:T(8,128)(2,1)S(1)} %bitcast.1, bf16[384,512]{1,0:T(8,128)(2,1)S(1)} %update_matrix.1.refs_1_, f32[512,128]{1,0:T(8,128)S(1)} %in_order.5.refs_2_, f32[512,128]{1,0:T(8,128)S(1)} %collective-permute-done.5.refs_0_.refs_3_, ...), custom_call_target="tpu_custom_call", output_to_operand_aliasing={{}: (6, {})} | custom-call | bytes 3000000 | tf_op jit(solution)/shard_map/update_far/pallas_call | solution.py:375
  59.6 1.1 %collective-permute-done.8.refs_2_ = f32[512,128]{1,0:T(8,128)S(1)} collective-permute-done((f32[512,128]{1,0:T(8,128)S(1)}, f32[512,128]{1,0:T(8,128)S(1)}, u32[]{:S(2)}, u32[]{:S(2)}) %collective-permute-start.8) | collective-permute-done | bytes 262176 | tf_op jit(solution)/shard_map/ppermute | solution.py:395
  60.7 1.7 %update_last.1 = f32[8192,512]{1,0:T(8,128)} custom-call(bf16[8192,512]{1,0:T(8,128)(2,1)S(1)} %bitcast.1, bf16[384,512]{1,0:T(8,128)(2,1)S(1)} %update_matrix.1.refs_1_, f32[512,128]{1,0:T(8,128)S(1)} %collective-permute-done.8.refs_2_, f32[8192,512]{1,0:T(8,128)} %update_far.1.refs_3_), custom_call_target="tpu_custom_call", output_to_operand_aliasing={{}: (3, {})} | custom-call | bytes 3000000 | tf_op jit(solution)/shard_map/update_last/pallas_call | solution.py:375
  (6 shorter events, 0.1 us)
Async XLA Ops:
  17.6 9.4 %collective-permute-start = (f32[1056,128]{1,0:T(8,128)S(1)}, f32[1056,128]{1,0:T(8,128)S(1)}, u32[]{:S(2)}, u32[]{:S(2)}) collective-permute-start(f32[1056,128]{1,0:T(8,128)S(1)} %given_first.1.mine_ref._), channel_id=1, source_target_pairs={{0,1},{1,0},{2,3},{3,2},{4,7},{5,6},{6,5},{7,4},{8,9},{9,8},{10,11... | collective-permute-start | bytes 1622024 | tf_op jit(solution)/shard_map/ppermute | solution.py:395
  19.6 3.4 %copy-start = (bf16[8192,512]{1,0:T(8,128)(2,1)S(1)}, bf16[8192,512]{1,0:T(8,128)(2,1)}, u32[]{:S(2)}) copy-start(bf16[8192,512]{1,0:T(8,128)(2,1)} %refs_0_.5) | copy-start | bytes 25165828
  23.7 11.6 %slice-start = ((s8[8388608]{0:T(1024)(128)(4,1)}), s8[4194304]{0:T(1024)(128)(4,1)S(1)}, s32[]{:S(2)}) async-start(s8[8388608]{0:T(1024)(128)(4,1)} %bitcast), calls=%async_computation.1 | async-start | bytes 8388608
  23.7 7.9 %collective-permute-start.2 = (f32[512,128]{1,0:T(8,128)S(1)}, f32[512,128]{1,0:T(8,128)S(1)}, u32[]{:S(2)}, u32[]{:S(2)}) collective-permute-start(f32[512,128]{1,0:T(8,128)S(1)} %get-tuple-element.13.mine_ref), channel_id=1, source_target_pairs={{0,1},{1,0},{2,3},{3,2},{4,7},{5,6},{6,5},{7,4},{8,9},{9,8},{10,11... | collective-permute-start | bytes 786440 | tf_op jit(solution)/shard_map/ppermute | solution.py:395
  27.5 7.8 %slice-start.1 = ((s8[8388608]{0:T(1024)(128)(4,1)}), s8[4194304]{0:T(1024)(128)(4,1)S(1)}, s32[]{:S(2)}) async-start(s8[8388608]{0:T(1024)(128)(4,1)} %bitcast), calls=%async_computation.2 | async-start | bytes 8388608
  27.5 8.7 %collective-permute-start.1 = (f32[544,128]{1,0:T(8,128)S(1)}, f32[544,128]{1,0:T(8,128)S(1)}, u32[]{:S(2)}, u32[]{:S(2)}) collective-permute-start(f32[544,128]{1,0:T(8,128)S(1)} %passed_products.2.sent_ref._), channel_id=1, source_target_pairs={{0,3},{1,2},{2,1},{3,0},{4,5},{5,4},{6,7},{7,6},{8,11},{9,10},{10,... | collective-permute-start | bytes 835592 | tf_op jit(solution)/shard_map/ppermute | solution.py:398
  32.5 9.1 %collective-permute-start.3 = (f32[512,128]{1,0:T(8,128)S(1)}, f32[512,128]{1,0:T(8,128)S(1)}, u32[]{:S(2)}, u32[]{:S(2)}) collective-permute-start(f32[512,128]{1,0:T(8,128)S(1)} %in_order.3), channel_id=1, source_target_pairs={{0,1},{1,0},{2,3},{3,2},{4,7},{5,6},{6,5},{7,4},{8,9},{9,8},{10,11... | collective-permute-start | bytes 786440 | tf_op jit(solution)/shard_map/ppermute | solution.py:395
  32.7 10.3 %collective-permute-start.4 = (f32[512,128]{1,0:T(8,128)S(1)}, f32[512,128]{1,0:T(8,128)S(1)}, u32[]{:S(2)}, u32[]{:S(2)}) collective-permute-start(f32[512,128]{1,0:T(8,128)S(1)} %passed_products.3._), channel_id=1, source_target_pairs={{0,3},{1,2},{2,1},{3,0},{4,5},{5,4},{6,7},{7,6},{8,11},{9,10},{10,... | collective-permute-start | bytes 786440 | tf_op jit(solution)/shard_map/ppermute | solution.py:398
  36.2 12.5 %collective-permute-start.6 = (f32[512,128]{1,0:T(8,128)S(1)}, f32[512,128]{1,0:T(8,128)S(1)}, u32[]{:S(2)}, u32[]{:S(2)}) collective-permute-start(f32[512,128]{1,0:T(8,128)S(1)} %added.2.refs_2_), channel_id=1, source_target_pairs={{0,3},{1,2},{2,1},{3,0},{4,5},{5,4},{6,7},{7,6},{8,11},{9,10},{10,... | collective-permute-start | bytes 786440 | tf_op jit(solution)/shard_map/ppermute | solution.py:398
  40.0 9.2 %collective-permute-start.5 = (f32[512,128]{1,0:T(8,128)S(1)}, f32[512,128]{1,0:T(8,128)S(1)}, u32[]{:S(2)}, u32[]{:S(2)}) collective-permute-start(f32[512,128]{1,0:T(8,128)S(1)} %added.2.refs_2_), channel_id=1, source_target_pairs={{0,1},{1,0},{2,3},{3,2},{4,7},{5,6},{6,5},{7,4},{8,9},{9,8},{10,11... | collective-permute-start | bytes 786440 | tf_op jit(solution)/shard_map/ppermute | solution.py:395
  43.1 11.2 %collective-permute-start.7 = (f32[512,128]{1,0:T(8,128)S(1)}, f32[512,128]{1,0:T(8,128)S(1)}, u32[]{:S(2)}, u32[]{:S(2)}) collective-permute-start(f32[512,128]{1,0:T(8,128)S(1)} %added.3.refs_3_), channel_id=1, source_target_pairs={{0,3},{1,2},{2,1},{3,0},{4,5},{5,4},{6,7},{7,6},{8,11},{9,10},{10,... | collective-permute-start | bytes 786440 | tf_op jit(solution)/shard_map/ppermute | solution.py:398
  45.8 8.9 %collective-permute-start.9 = (f32[512,128]{1,0:T(8,128)S(1)}, f32[512,128]{1,0:T(8,128)S(1)}, u32[]{:S(2)}, u32[]{:S(2)}) collective-permute-start(f32[512,128]{1,0:T(8,128)S(1)} %added.3.refs_3_), channel_id=1, source_target_pairs={{0,1},{1,0},{2,3},{3,2},{4,7},{5,6},{6,5},{7,4},{8,9},{9,8},{10,11... | collective-permute-start | bytes 786440 | tf_op jit(solution)/shard_map/ppermute | solution.py:395
  49.2 6.6 %collective-permute-start.10 = (f32[512,128]{1,0:T(8,128)S(1)}, f32[512,128]{1,0:T(8,128)S(1)}, u32[]{:S(2)}, u32[]{:S(2)}) collective-permute-start(f32[512,128]{1,0:T(8,128)S(1)} %in_order.4.refs_4_), channel_id=1, source_target_pairs={{0,1},{1,0},{2,3},{3,2},{4,7},{5,6},{6,5},{7,4},{8,9},{9,8},{10,11... | collective-permute-start | bytes 786440 | tf_op jit(solution)/shard_map/ppermute | solution.py:395
  54.3 6.4 %collective-permute-start.8 = (f32[512,128]{1,0:T(8,128)S(1)}, f32[512,128]{1,0:T(8,128)S(1)}, u32[]{:S(2)}, u32[]{:S(2)}) collective-permute-start(f32[512,128]{1,0:T(8,128)S(1)} %in_order.5.refs_2_), channel_id=1, source_target_pairs={{0,1},{1,0},{2,3},{3,2},{4,7},{5,6},{6,5},{7,4},{8,9},{9,8},{10,11... | collective-permute-start | bytes 786440 | tf_op jit(solution)/shard_map/ppermute | solution.py:395
